TPU v7x, 32 devices: a whole 2x2x4 slice. The times are simulated.
32 devices in a mesh: groups: 2 (over x), req: 16 (over z, y, core).
Axes of the slice: x: 2, y: 2, z: 4, core: 2. Of those that a mesh axis runs over, the one named last changes fastest.
Arguments:
- normed_hidden: bfloat16 [6144, 8192], P(('groups', 'req')), parts along dimension 0, may hold values from -6 to 6
- attn_mixed: bfloat16 [6144, 8192], P(('groups', 'req')), parts along dimension 0, may hold values from -6 to 6
- adapter_ids: int32 [6144], P(('groups', 'req')), parts along dimension 0, may hold values from 0 to 15, as said below
- send_slot: int32 [6144], P(('groups', 'req')), parts along dimension 0, may hold values from 0 to 383, as said below
- padded_row: int32 [6144], P(('groups', 'req')), parts along dimension 0, may hold values from 0 to 510, as said below
- fetch_list: int32 [32, 2], P('groups'), parts along dimension 0, may hold values from 0 to 15, as said below
- shrink_panels: bfloat16 [16, 256, 8192], P(None, None, 'req'), may hold values from -0.0625 to 0.0625
- expand_qo: bfloat16 [16, 128, 8192], P(None, None, 'req'), may hold values from -0.75 to 0.75
- expand_kv: bfloat16 [16, 128, 1024], P(None, None, 'req'), may hold values from -0.75 to 0.75
Outputs:
- delta_q: bfloat16 [6144, 8192], P(('groups', 'req')), parts along dimension 0
- delta_k: bfloat16 [6144, 1024], P(('groups', 'req')), parts along dimension 0
- delta_v: bfloat16 [6144, 1024], P(('groups', 'req')), parts along dimension 0
- delta_o: bfloat16 [6144, 8192], P(('groups', 'req')), parts along dimension 0
There are 2 independent parts, one for each index of `groups`. A program takes and returns all parts, laid end to end along the dimension named above; an argument that names none is the same for every part. Nothing has to cross between parts.
Inputs may be any that keep to these rules, and one draw needn't show every extreme that they name: `adapter_ids`: within one owner the tokens of each block of 128 rows name one adapter. `send_slot`: slots of one device's tokens are distinct; at most 24 tokens of one device go to one owner, and some owner receives 24 tokens from every device. `padded_row`: rows of one owner's tokens are distinct. `fetch_list`: each owner's list holds 2 different adapters.
All inputs are finite; a program needn't handle non-finite values.
Results may differ from a plain program's by a relative error of at most 0.0051.
Values may be sent and summed in bfloat16 or wider, within the bound.
No kernel may reach another device: no remote copies, remote signals or barrier semaphores. Data moves between devices by JAX's collectives and lax.ppermute only.
A program may use at most 192 MiB of HBM per device.

v0:
```python
import jax
import jax.numpy as jnp
from jax import lax
from jax.sharding import PartitionSpec as P

BLK = 128


adapter_scale_factor = 2.0


def expand_part(shrunk_part, panel_part):
    final_deltas = jnp.einsum(
        "bnr,brc->bnc", shrunk_part, panel_part, preferred_element_type=jnp.float32
    )
    return (adapter_scale_factor * final_deltas).astype(jnp.bfloat16)


def pack_rows(
    normed_hidden, attn_mixed, adapter_ids, send_slot, padded_row, devices, slot_rows, capacity
):
    send_rows = devices * slot_rows
    model_width = normed_hidden.shape[1]
    out_x = jnp.zeros((send_rows, model_width), jnp.bfloat16).at[send_slot].set(normed_hidden)
    out_y = jnp.zeros((send_rows, model_width), jnp.bfloat16).at[send_slot].set(attn_mixed)
    out_rows = jnp.full((send_rows,), capacity, jnp.int32).at[send_slot].set(padded_row)
    out_ids = jnp.full((send_rows,), -1, jnp.int32).at[send_slot].set(adapter_ids)
    return (
        out_x.reshape(devices, slot_rows, model_width),
        out_y.reshape(devices, slot_rows, model_width),
        out_rows.reshape(devices, slot_rows),
        out_ids.reshape(devices, slot_rows),
    )


def owner_shrink(in_x, in_y, in_rows, in_ids, panels_a, own_list, capacity, rank_width):
    devices, slot_rows, model_width = in_x.shape
    send_rows = devices * slot_rows
    block_total = capacity // BLK
    in_rows = in_rows.reshape(send_rows)
    in_ids = in_ids.reshape(send_rows)
    buffer_x = (
        jnp.zeros((capacity, model_width), jnp.bfloat16)
        .at[in_rows]
        .set(in_x.reshape(send_rows, model_width), mode="drop")
    )
    buffer_y = (
        jnp.zeros((capacity, model_width), jnp.bfloat16)
        .at[in_rows]
        .set(in_y.reshape(send_rows, model_width), mode="drop")
    )
    row_ids = jnp.full((capacity,), -1, jnp.int32).at[in_rows].max(in_ids, mode="drop")
    block_adapter = jnp.max(row_ids.reshape(block_total, BLK), axis=1)
    matches = block_adapter[:, None] == own_list[None, :]
    listed = jnp.any(matches, axis=1) & (block_adapter >= 0)
    block_slot = jnp.argmax(matches, axis=1)
    chosen = panels_a[block_slot]
    shrink_x = jnp.einsum(
        "bnd,brd->bnr",
        buffer_x.reshape(block_total, BLK, model_width),
        chosen[:, : 3 * rank_width],
        preferred_element_type=jnp.float32,
    )
    shrink_y = jnp.einsum(
        "bnd,brd->bnr",
        buffer_y.reshape(block_total, BLK, model_width),
        chosen[:, 3 * rank_width :],
        preferred_element_type=jnp.float32,
    )
    keeper = listed.astype(jnp.float32)[:, None, None]
    reduced_rows = (jnp.concatenate([shrink_x, shrink_y], axis=2) * keeper).astype(jnp.bfloat16)
    return (reduced_rows, block_adapter, block_slot, in_rows)


def shards(
    normed_hidden,
    attn_mixed,
    adapter_ids,
    send_slot,
    padded_row,
    fetch_list,
    shrink_panels,
    expand_qo,
    expand_kv,
):
    devices = lax.axis_size("req")
    own_index = lax.axis_index("req")
    tok_rows, model_width = normed_hidden.shape
    rank_width = shrink_panels.shape[1] // 4
    fetch_count = fetch_list.shape[1]
    slot_rows = 2 * tok_rows // devices
    capacity = 2 * tok_rows + (fetch_count - 1) * BLK
    send_rows = devices * slot_rows
    own_list = fetch_list[own_index]
    got_a, got_qo, got_kv = (
        lax.all_to_all(shrink_panels[fetch_list], "req", split_axis=0, concat_axis=3, tiled=True),
        lax.all_to_all(expand_qo[fetch_list], "req", split_axis=0, concat_axis=3, tiled=True),
        lax.all_to_all(expand_kv[fetch_list], "req", split_axis=0, concat_axis=3, tiled=True),
    )
    packed = pack_rows(
        normed_hidden, attn_mixed, adapter_ids, send_slot, padded_row, devices, slot_rows, capacity
    )
    in_x, in_y, in_rows, in_ids = (
        lax.all_to_all(packed[0], "req", split_axis=0, concat_axis=0, tiled=True),
        lax.all_to_all(packed[1], "req", split_axis=0, concat_axis=0, tiled=True),
        lax.all_to_all(packed[2], "req", split_axis=0, concat_axis=0, tiled=True),
        lax.all_to_all(packed[3], "req", split_axis=0, concat_axis=0, tiled=True),
    )
    reduced_rows, block_adapter, block_slot, flat_rows = owner_shrink(
        in_x, in_y, in_rows, in_ids, got_a[0], own_list, capacity, rank_width
    )
    query_output_pair = got_qo[0][block_slot]
    key_value_pair = got_kv[0][block_slot]
    query_portion = expand_part(
        reduced_rows[:, :, :rank_width], query_output_pair[:, :rank_width]
    ).reshape(capacity, -1)
    key_portion = expand_part(
        reduced_rows[:, :, rank_width : 2 * rank_width], key_value_pair[:, :rank_width]
    ).reshape(capacity, -1)
    value_portion = expand_part(
        reduced_rows[:, :, 2 * rank_width : 3 * rank_width], key_value_pair[:, rank_width:]
    ).reshape(capacity, -1)
    output_portion = expand_part(
        reduced_rows[:, :, 3 * rank_width :], query_output_pair[:, rank_width:]
    ).reshape(capacity, -1)
    back_rows = jnp.minimum(flat_rows, capacity - 1)
    home_q, home_k, home_v, home_o = (
        lax.all_to_all(
            query_portion[back_rows].reshape(devices, slot_rows, -1),
            "req",
            split_axis=0,
            concat_axis=0,
            tiled=True,
        ),
        lax.all_to_all(
            key_portion[back_rows].reshape(devices, slot_rows, -1),
            "req",
            split_axis=0,
            concat_axis=0,
            tiled=True,
        ),
        lax.all_to_all(
            value_portion[back_rows].reshape(devices, slot_rows, -1),
            "req",
            split_axis=0,
            concat_axis=0,
            tiled=True,
        ),
        lax.all_to_all(
            output_portion[back_rows].reshape(devices, slot_rows, -1),
            "req",
            split_axis=0,
            concat_axis=0,
            tiled=True,
        ),
    )
    delta_q = home_q.reshape(send_rows, -1)[send_slot]
    delta_k = home_k.reshape(send_rows, -1)[send_slot]
    delta_v = home_v.reshape(send_rows, -1)[send_slot]
    delta_o = home_o.reshape(send_rows, -1)[send_slot]
    return (delta_q, delta_k, delta_v, delta_o)


def solution(mesh):
    in_specs = (
        P(("groups", "req"), None),
        P(("groups", "req"), None),
        P(("groups", "req")),
        P(("groups", "req")),
        P(("groups", "req")),
        P("groups", None),
        P(None, None, "req"),
        P(None, None, "req"),
        P(None, None, "req"),
    )
    out_specs = (
        P(("groups", "req"), None),
        P(("groups", "req"), None),
        P(("groups", "req"), None),
        P(("groups", "req"), None),
    )
    return jax.shard_map(shards, mesh=mesh, in_specs=in_specs, out_specs=out_specs, check_vma=False)
```

profile of v0, /device:TPU:15, one launch (start us, length us, event | category | flops | bytes accessed | tf_op | source)
XLA Modules:
  0.0 1014.7 jit_solution(707142376588698975)
XLA Ops:
  3.5 6.6 all-to-all-start
  23.6 6.1 all-to-all-start.7
  29.7 9.7 scatter_custom_fusion.1
  43.3 6.0 all-to-all-start.1
  49.4 9.7 scatter_custom_fusion.5
  59.1 127.6 %all-to-all-done.1 = bf16[16,24,8192]{2,1,0:T(8,128)(2,1)} async-done(((bf16[16,24,8192]{2,1,0:T(8,128)(2,1)}), bf16[16,24,8192]{2,1,0:T(8,128)(2,1)}, u32[]{:S(2)}, u32[]{:S(2)}) %all-to-all-start.1) | async-done | bytes 6291488 | tf_op jit(solution)/shard_map/all_to_all | solution.py:104
  191.5 7.2 gather_fusion
  198.7 130.2 %all-to-all-done.4 = bf16[16,24,8192]{2,1,0:T(8,128)(2,1)} async-done(((bf16[16,24,8192]{2,1,0:T(8,128)(2,1)}), bf16[16,24,8192]{2,1,0:T(8,128)(2,1)}, u32[]{:S(2)}, u32[]{:S(2)}) %all-to-all-start.4) | async-done | bytes 6291488 | tf_op jit(solution)/shard_map/all_to_all | solution.py:105
  336.6 179.6 %all-to-all-done.2 = bf16[16,2,256,512]{3,2,1,0:T(8,128)(2,1)} async-done(((bf16[16,2,256,512]{3,2,1,0:T(8,128)(2,1)}), bf16[16,2,256,512]{3,2,1,0:T(8,128)(2,1)}, u32[]{:S(2)}, u32[]{:S(2)}) %all-to-all-start.2) | async-done | bytes 8388640 | tf_op jit(solution)/shard_map/all_to_all | solution.py:96
  529.3 15.6 %scatter_custom_fusion.2 = bf16[512,8192]{1,0:T(8,128)(2,1)} fusion(s32[384]{0:T(512)S(1)} %get-tuple-element.7, bf16[384,8192]{1,0:T(8,128)(2,1)} %bitcast.1, bf16[]{:T(256)} %constant.12.clone.1), kind=kCustom, calls=%fused_computation.34 | custom fusion | bytes 8389120 | tf_op jit(solution)/shard_map/scatter | solution.py:45
  544.9 15.8 %scatter_custom_fusion.6 = bf16[512,8192]{1,0:T(8,128)(2,1)} fusion(s32[384]{0:T(512)S(1)} %get-tuple-element.7, bf16[384,8192]{1,0:T(8,128)(2,1)} %bitcast.9, bf16[]{:T(256)} %constant.12.clone.1), kind=kCustom, calls=%fused_computation.32 | custom fusion | bytes 8389120 | tf_op jit(solution)/shard_map/scatter | solution.py:50
  560.7 11.9 %copy.26 = bf16[1,2,256,16,512]{2,4,3,1,0:T(8,128)(2,1)} copy(bf16[1,2,256,16,512]{4,2,1,3,0:T(8,128)(2,1)} %bitcast.5) | data formatting | bytes 16777216 | tf_op jit(solution)/shard_map/all_to_all | solution.py:96
  624.1 7.6 fusion.4
  631.7 10.7 %fusion = f32[4,128,192]{1,2,0:T(8,128)S(1)} fusion(bf16[4,128,8192]{2,1,0:T(8,128)(2,1)} %bitcast.54, bf16[4,256,8192]{2,1,0:T(8,128)(2,1)} %constant_dynamic-update-slice_fusion), kind=kOutput, calls=%fused_computation.26 | convolution fusion | flops 1610612736 | bytes 21364736 | tf_op jit(solution)/shard_map/bnd,brd->bnr/dot_general | solution.py:58
  645.8 6.3 all-to-all-start.8
  652.1 6.2 copy.31
  698.3 19.3 %gather_fusion.10 = bf16[384,8192]{1,0:T(8,128)(2,1)} fusion(bf16[512,8192]{1,0:T(8,128)(2,1)} %bitcast.38, s32[1024]{0:T(1024)S(1)} %get-tuple-element.14), kind=kCustom, calls=%fused_computation.10 | custom fusion | bytes 12584448 | tf_op jit(solution)/shard_map/gather | solution.py:150
  717.6 6.6 all-to-all-start.10
  724.2 7.8 multiply_convert_fusion.1
  732.0 19.3 %gather_fusion.2 = bf16[384,8192]{1,0:T(8,128)(2,1)} fusion(bf16[512,8192]{1,0:T(8,128)(2,1)} %bitcast.37, s32[1024]{0:T(1024)S(1)} %get-tuple-element.14), kind=kCustom, calls=%fused_computation.2 | custom fusion | bytes 12584448 | tf_op jit(solution)/shard_map/gather | solution.py:129
  751.3 110.2 %all-to-all-done.10 = bf16[16,24,8192]{2,1,0:T(8,128)(2,1)} async-done(((bf16[16,24,8192]{2,1,0:T(8,128)(2,1)}), bf16[16,24,8192]{2,1,0:T(8,128)(2,1)}, u32[]{:S(2)}, u32[]{:S(2)}) %all-to-all-start.10) | async-done | bytes 6291488 | tf_op jit(solution)/shard_map/all_to_all | solution.py:149
  870.0 10.6 %gather_fusion.11 = bf16[192,8192]{1,0:T(8,128)(2,1)} fusion(bf16[384,8192]{1,0:T(8,128)(2,1)} %bitcast.30, s32[1024]{0:T(1024)S(1)} %pad_clamp_fusion), kind=kCustom, calls=%fused_computation.11 | custom fusion | bytes 6292224 | tf_op jit(solution)/shard_map/gather | solution.py:160
  880.7 123.1 %all-to-all-done.6 = bf16[16,24,8192]{2,1,0:T(8,128)(2,1)} async-done(((bf16[16,24,8192]{2,1,0:T(8,128)(2,1)}), bf16[16,24,8192]{2,1,0:T(8,128)(2,1)}, u32[]{:S(2)}, u32[]{:S(2)}) %all-to-all-start.6) | async-done | bytes 6291488 | tf_op jit(solution)/shard_map/all_to_all | solution.py:128
  1003.7 10.8 %gather_fusion.3 = bf16[192,8192]{1,0:T(8,128)(2,1)} fusion(bf16[384,8192]{1,0:T(8,128)(2,1)} %bitcast.17, s32[1024]{0:T(1024)S(1)} %pad_clamp_fusion), kind=kCustom, calls=%fused_computation.3 | custom fusion | bytes 6292224 | tf_op jit(solution)/shard_map/gather | solution.py:157
  (83 shorter events, 149.3 us)
Async XLA Ops:
  0.6 333.2 %copy-start = (bf16[16,128,512]{2,1,0:T(8,128)(2,1)S(1)}, bf16[16,128,512]{2,1,0:T(8,128)(2,1)}, u32[]{:S(2)}) copy-start(bf16[16,128,512]{2,1,0:T(8,128)(2,1)} %param.16) | copy-start | bytes 6291460
  3.5 10.3 %all-to-all-start = ((s32[16,1,24]{2,1,0:T(1,128)}), s32[16,1,24]{2,1,0:T(1,128)S(1)}, u32[]{:S(2)}, u32[]{:S(2)}) async-start(s32[16,1,24]{2,1,0:T(1,128)} %all_to_all.63), calls=%async_computation | async-start | bytes 16384 | tf_op jit(solution)/shard_map/all_to_all | solution.py:106
  13.8 9.8 all-to-all-start.3
  23.6 19.7 %all-to-all-start.7 = ((bf16[16,2,128,64]{2,3,1,0:T(8,128)(2,1)}), bf16[16,2,128,64]{2,3,1,0:T(8,128)(2,1)S(1)}, u32[]{:S(2)}, u32[]{:S(2)}) async-start(bf16[16,2,128,64]{2,3,1,0:T(8,128)(2,1)} %bitcast.18), calls=%async_computation.7 | async-start | bytes 1048576 | tf_op jit(solution)/shard_map/all_to_all | solution.py:98
  43.3 143.3 %all-to-all-start.1 = ((bf16[16,24,8192]{2,1,0:T(8,128)(2,1)}), bf16[16,24,8192]{2,1,0:T(8,128)(2,1)}, u32[]{:S(2)}, u32[]{:S(2)}) async-start(bf16[16,24,8192]{2,1,0:T(8,128)(2,1)} %bitcast.44), calls=%async_computation.1 | async-start | bytes 12582912 | tf_op jit(solution)/shard_map/all_to_all | solution.py:104
  186.6 142.3 %all-to-all-start.4 = ((bf16[16,24,8192]{2,1,0:T(8,128)(2,1)}), bf16[16,24,8192]{2,1,0:T(8,128)(2,1)}, u32[]{:S(2)}, u32[]{:S(2)}) async-start(bf16[16,24,8192]{2,1,0:T(8,128)(2,1)} %bitcast.45), calls=%async_computation.4 | async-start | bytes 12582912 | tf_op jit(solution)/shard_map/all_to_all | solution.py:105
  328.9 187.3 %all-to-all-start.2 = ((bf16[16,2,256,512]{3,2,1,0:T(8,128)(2,1)}), bf16[16,2,256,512]{3,2,1,0:T(8,128)(2,1)}, u32[]{:S(2)}, u32[]{:S(2)}) async-start(bf16[16,2,256,512]{3,2,1,0:T(8,128)(2,1)} %bitcast.43), calls=%async_computation.2 | async-start | bytes 16777216 | tf_op jit(solution)/shard_map/all_to_all | solution.py:96
  336.6 184.5 %copy-start.4 = (s32[16,2]{0,1:T(2,128)S(1)}, s32[16,2]{0,1:T(2,128)}, u32[]{:S(2)}) copy-start(s32[16,2]{0,1:T(2,128)} %param.14) | copy-start | bytes 388
  516.2 129.6 %all-to-all-start.5 = ((bf16[16,2,128,512]{3,2,1,0:T(8,128)(2,1)}), bf16[16,2,128,512]{3,2,1,0:T(8,128)(2,1)}, u32[]{:S(2)}, u32[]{:S(2)}) async-start(bf16[16,2,128,512]{3,2,1,0:T(8,128)(2,1)} %bitcast.52), calls=%async_computation.5 | async-start | bytes 8388608 | tf_op jit(solution)/shard_map/all_to_all | solution.py:97
  610.4 11.1 %slice-start = ((s8[5242880]{0:T(1024)(128)(4,1)}), s8[4194304]{0:T(1024)(128)(4,1)S(1)}, s32[]{:S(2)}) async-start(s8[5242880]{0:T(1024)(128)(4,1)} %bitcast.48), calls=%async_computation.11 | async-start | bytes 8388608
  615.9 5.6 slice-start.1
  645.8 37.1 %all-to-all-start.8 = ((bf16[16,24,1024]{2,1,0:T(8,128)(2,1)}), bf16[16,24,1024]{2,1,0:T(8,128)(2,1)S(1)}, u32[]{:S(2)}, u32[]{:S(2)}) async-start(bf16[16,24,1024]{2,1,0:T(8,128)(2,1)} %bitcast.56), calls=%async_computation.8 | async-start | bytes 1572864 | tf_op jit(solution)/shard_map/all_to_all | solution.py:135
  682.9 34.7 %all-to-all-start.9 = ((bf16[16,24,1024]{2,1,0:T(8,128)(2,1)}), bf16[16,24,1024]{2,1,0:T(8,128)(2,1)S(1)}, u32[]{:S(2)}, u32[]{:S(2)}) async-start(bf16[16,24,1024]{2,1,0:T(8,128)(2,1)} %bitcast.26), calls=%async_computation.9 | async-start | bytes 1572864 | tf_op jit(solution)/shard_map/all_to_all | solution.py:142
  688.9 3.4 copy-start.3
  692.6 5.7 copy-start.2
  717.6 143.8 %all-to-all-start.10 = ((bf16[16,24,8192]{2,1,0:T(8,128)(2,1)}), bf16[16,24,8192]{2,1,0:T(8,128)(2,1)}, u32[]{:S(2)}, u32[]{:S(2)}) async-start(bf16[16,24,8192]{2,1,0:T(8,128)(2,1)} %bitcast.47), calls=%async_computation.10 | async-start | bytes 12582912 | tf_op jit(solution)/shard_map/all_to_all | solution.py:149
  861.4 142.3 %all-to-all-start.6 = ((bf16[16,24,8192]{2,1,0:T(8,128)(2,1)}), bf16[16,24,8192]{2,1,0:T(8,128)(2,1)}, u32[]{:S(2)}, u32[]{:S(2)}) async-start(bf16[16,24,8192]{2,1,0:T(8,128)(2,1)} %bitcast.46), calls=%async_computation.6 | async-start | bytes 12582912 | tf_op jit(solution)/shard_map/all_to_all | solution.py:128
  1003.7 10.8 %copy-start.1 = (bf16[16,128,512]{2,1,0:T(8,128)(2,1)S(1)}, bf16[16,128,512]{2,1,0:T(8,128)(2,1)}, u32[]{:S(2)}) copy-start(bf16[16,128,512]{2,1,0:T(8,128)(2,1)} %param.16) | copy-start | bytes 6291460
where the time goes:
time: 1020 us; the launch traced here: 1010 us
  waiting for transfers between devices  677 us (66%)
  local copies, waits for them, and re-layouts  233 us (23%)
  starting transfers between devices  63.3 us (6%)
  matrix products  32.8 us (3%)
    all_to_all x1, waiting for transfers between devices, shards(): lax.all_to_all(shrink_panels[fetch_list], 'req', split_axis=0, concat_axi...  180 us
    all_to_all x1, waiting for transfers between devices, shards(): lax.all_to_all(packed[1], 'req', split_axis=0, concat_axis=0, tiled=True)  130 us
    all_to_all x1, waiting for transfers between devices, shards(): lax.all_to_all(packed[0], 'req', split_axis=0, concat_axis=0, tiled=True)  128 us
    all_to_all x1, waiting for transfers between devices, shards(): lax.all_to_all(query_portion[back_rows].reshape(devices, slot_rows, -1),...  123 us
    all_to_all x1, waiting for transfers between devices, shards(): lax.all_to_all(output_portion[back_rows].reshape(devices, slot_rows, -1),...  110 us
    unnamed x24, local copies, waits for them, and re-layouts  39.1 us
    gather x5, local copies, waits for them, and re-layouts, owner_shrink(): chosen = panels_a[block_slot]  24.3 us
  transfers between devices with their start and end apart: 11, of which 8 were waited for; matrix products, arithmetic and copies ran while one was open for 25% of the time, Pallas kernels for 0%

commit v1 on v0

v1 whole, which is shorter than its diff:
```python
import functools

import jax
import jax.numpy as jnp
from jax import lax
from jax.experimental import pallas as pl
from jax.experimental.pallas import tpu as pltpu
from jax.sharding import Mesh, PartitionSpec as P

LANES = 128
SET = 8
RANK = 64
SCALE = 2.0
VMEM_LIMIT = 48 * 1024 * 1024
PLANE = ("groups", "r")


def nt_dot(left, right):
    return lax.dot_general(
        left, right, (((1,), (1,)), ((), ())), preferred_element_type=jnp.float32
    )


def piece_offset(h, k, count, width):
    if count == 1:
        return 0
    start = lax.rem(h - k + count, count) * width
    return pl.multiple_of(start, LANES)


def shrink_kernel(ids_ref, tokens_ref, *rest):
    piece_refs, out_ref = rest[:-1], rest[-1]
    adapters, ranks, width = piece_refs[0].shape
    ids = ids_ref[...]
    pair_of = ids >> 1
    wide = jnp.zeros((tokens_ref.shape[0], 2 * ranks), jnp.float32)
    for first in range(0, adapters, 4):
        part = None
        for k, piece in enumerate(piece_refs):
            panel = piece[first : first + 4].reshape(4 * ranks, width)
            term = nt_dot(tokens_ref[:, k * width : (k + 1) * width], panel)
            part = term if part is None else part + term
        for j in range(2):
            wide = jnp.where(
                pair_of == first // 2 + j,
                part[:, 2 * j * ranks : 2 * (j + 1) * ranks],
                wide,
            )
    odd = (ids & 1) == 1
    out_ref[...] = jnp.where(odd, wide[:, ranks:], wide[:, :ranks]).astype(out_ref.dtype)


def shrink(ids, tokens, pieces, tile):
    rows, columns = tokens.shape
    adapters, ranks, width = pieces[0].shape
    return pl.pallas_call(
        shrink_kernel,
        grid=(rows // tile,),
        in_specs=[
            pl.BlockSpec((tile, 1), lambda i: (i, 0)),
            pl.BlockSpec((tile, columns), lambda i: (i, 0)),
        ]
        + [pl.BlockSpec((adapters, ranks, width), lambda i: (0, 0, 0))] * len(pieces),
        out_specs=pl.BlockSpec((tile, ranks), lambda i: (i, 0)),
        out_shape=jax.ShapeDtypeStruct((rows, ranks), jnp.bfloat16),
        compiler_params=pltpu.CompilerParams(vmem_limit_bytes=VMEM_LIMIT),
        cost_estimate=pl.CostEstimate(
            flops=2 * rows * columns * ranks * adapters,
            bytes_accessed=2 * (rows + adapters * ranks) * columns,
            transcendentals=0,
        ),
        name="shrink",
    )(ids, tokens, *pieces)


def expand_kernel(ids_ref, low_ref, *rest):
    piece_refs, out_ref = rest[:-1], rest[-1]
    adapters, ranks, width = piece_refs[0].shape
    ids = ids_ref[...]
    low = low_ref[...]
    spread = jnp.concatenate([low] * adapters, axis=1)
    lane_adapter = lax.broadcasted_iota(jnp.int32, spread.shape, 1) // ranks
    spread = jnp.where(lane_adapter == ids, spread, jnp.zeros_like(spread))
    for k, piece in enumerate(piece_refs):
        panel = piece[...].reshape(adapters * ranks, width)
        full = jnp.dot(spread, panel, preferred_element_type=jnp.float32)
        out_ref[:, k * width : (k + 1) * width] = (SCALE * full).astype(out_ref.dtype)


def expand(ids, low, pieces, tile):
    rows, ranks = low.shape
    adapters, _, width = pieces[0].shape
    columns = width * len(pieces)
    return pl.pallas_call(
        expand_kernel,
        grid=(rows // tile,),
        in_specs=[
            pl.BlockSpec((tile, 1), lambda i: (i, 0)),
            pl.BlockSpec((tile, ranks), lambda i: (i, 0)),
        ]
        + [pl.BlockSpec((adapters, ranks, width), lambda i: (0, 0, 0))] * len(pieces),
        out_specs=pl.BlockSpec((tile, columns), lambda i: (i, 0)),
        out_shape=jax.ShapeDtypeStruct((rows, columns), jnp.bfloat16),
        compiler_params=pltpu.CompilerParams(vmem_limit_bytes=VMEM_LIMIT),
        cost_estimate=pl.CostEstimate(
            flops=2 * rows * columns * ranks * adapters,
            bytes_accessed=2 * (rows + adapters * ranks) * columns,
            transcendentals=0,
        ),
        name="expand",
    )(ids, low, *pieces)


def exchange(array):
    return lax.all_to_all(array, PLANE, split_axis=0, concat_axis=0, tiled=True)


def ring(array, count):
    pieces = [array]
    order = [(k, (k + 1) % count) for k in range(count)]
    for _ in range(count - 1):
        pieces.append(lax.ppermute(pieces[-1], "h", order))
    return pieces


def in_lanes(pieces):
    if pieces[0].shape[2] % LANES == 0:
        return pieces
    return [jnp.concatenate(pieces, axis=2)]


def relative(h, count):
    return lax.rem(h - jnp.arange(count) + count, count)


def pack(array, h, count, inner, groups):
    rows, columns = array.shape
    width = columns // (count * inner * groups)
    cut = array.reshape(rows, count, inner, groups, width)
    cut = cut[:, relative(h, count)]
    return cut.transpose(3, 2, 0, 1, 4).reshape(groups * inner, rows, count * width)


def unpack(array, h, count, inner, groups):
    rows = array.shape[1]
    width = array.shape[2] // count
    cut = array.reshape(groups, inner, rows, count, width).transpose(2, 3, 1, 0, 4)
    cut = cut[:, relative(h, count)]
    return cut.reshape(rows, count * inner * groups * width)


def shards(
    normed_hidden,
    attn_mixed,
    adapter_ids,
    send_slot,
    padded_row,
    fetch_list,
    shrink_panels,
    expand_qo,
    expand_kv,
):
    groups, count, inner = (lax.axis_size(a) for a in ("groups", "h", "r"))
    g, h = lax.axis_index("groups"), lax.axis_index("h")
    devices = count * inner
    members = groups * inner
    tok_rows = normed_hidden.shape[0]
    slot_rows = 2 * tok_rows // devices
    rows = members * tok_rows
    tile = 2 * tok_rows

    listed = fetch_list[send_slot // slot_rows]
    keep = jnp.any(listed == adapter_ids[:, None], axis=1)
    own_ids = jnp.where(keep, adapter_ids, -1)
    ids = exchange(jnp.broadcast_to(own_ids, (members, tok_rows))).reshape(rows, 1)

    def own_columns(panel):
        width = panel.shape[2] // groups
        return lax.dynamic_slice_in_dim(panel, g * width, width, 2)

    panel_a = own_columns(shrink_panels)
    panel_b = own_columns(expand_qo)
    if groups == 2:
        panel_kv = lax.dynamic_slice_in_dim(expand_kv, g * RANK, RANK, 1)
    else:
        panel_kv = own_columns(expand_kv)
    a_o = in_lanes(ring(panel_a[:, 3 * RANK :], count))
    a_qkv = in_lanes(ring(panel_a[:, : 3 * RANK], count))
    b_kv = in_lanes(ring(panel_kv, count))
    b_q = in_lanes(ring(panel_b[:, :RANK], count))
    b_o = in_lanes(ring(panel_b[:, RANK:], count))

    def low_rows(tokens, pieces):
        sent = exchange(pack(tokens, h, count, inner, groups))
        part = shrink(ids, sent.reshape(rows, -1), pieces, tile)
        parts = exchange(part.reshape(members, tok_rows, -1))
        low = jnp.sum(parts.astype(jnp.float32), axis=0).astype(jnp.bfloat16)
        return lax.all_gather(low, PLANE, axis=0, tiled=True)

    def home(low, pieces):
        full = expand(ids, low, pieces, tile)
        return exchange(full.reshape(members, tok_rows, -1))

    low_o = low_rows(attn_mixed, a_o)
    low_qkv = low_rows(normed_hidden, a_qkv)
    low_k, low_v = low_qkv[:, RANK : 2 * RANK], low_qkv[:, 2 * RANK :]
    if groups == 2:
        both = home(jnp.where(g == 0, low_k, low_v), b_kv)
        half = both.reshape(2, inner, tok_rows, -1)
        delta_k = unpack(half[0], h, count, inner, 1)
        delta_v = unpack(half[1], h, count, inner, 1)
    else:
        panel = b_kv[0]
        delta_k = unpack(home(low_k, [panel[:, :RANK]]), h, count, inner, groups)
        delta_v = unpack(home(low_v, [panel[:, RANK:]]), h, count, inner, groups)
    delta_q = unpack(home(low_qkv[:, :RANK], b_q), h, count, inner, groups)
    delta_o = unpack(home(low_o, b_o), h, count, inner, groups)
    return delta_q, delta_k, delta_v, delta_o


def solution(mesh):
    groups, devices = mesh.devices.shape
    inner = max(SET // groups, 1)
    cut = Mesh(mesh.devices.reshape(groups, devices // inner, inner), ("groups", "h", "r"))
    by_token = P(("groups", "h", "r"))
    by_token_rows = P(("groups", "h", "r"), None)
    by_column = P(None, None, ("h", "r"))
    in_specs = (
        (by_token_rows,) * 2 + (by_token,) * 3 + (P("groups", None),) + (by_column,) * 3
    )
    out_specs = (by_token_rows,) * 4
    return jax.shard_map(shards, mesh=cut, in_specs=in_specs, out_specs=out_specs, check_vma=False)
```

time: 1020 us -> 436 us (0.43)
  the two profiles are of different devices: /device:TPU:15 before, /device:TPU:0 now
where the time goes in v1:
time: 436 us; the launch traced here: 433 us
  waiting for transfers between devices  185 us (42%)
  local copies, waits for them, and re-layouts  129 us (30%)
  starting transfers between devices  49.5 us (11%)
  Pallas kernels  36.5 us (8%)
  blocking collectives  26.3 us (6%)
  other arithmetic  5.1 us (1%)
    ppermute x15, waiting for transfers between devices, ring(): pieces.append(lax.ppermute(pieces[-1], 'h', order))  180 us
    all_to_all x8, starting transfers between devices, exchange(): return lax.all_to_all(array, PLANE, split_axis=0, concat_axis=0, tiled=True)  45.6 us
    all_gather x2, blocking collectives, low_rows(): return lax.all_gather(low, PLANE, axis=0, tiled=True)  26.3 us
    gather x6, local copies, waits for them, and re-layouts, unpack(): cut = cut[:, relative(h, count)]  23.5 us
    pallas_call x2, Pallas kernels, shrink(): pl.pallas_call(shrink_kernel, grid=(rows // tile,), in_specs=[pl.BlockSpe...  21 us
    gather x2, local copies, waits for them, and re-layouts, pack(): cut = cut[:, relative(h, count)]  20.2 us
    reshape x4, local copies, waits for them, and re-layouts, unpack(): array.reshape(groups, inner, rows, count, width).transpose(2, 3, 1, 0, 4)  16.6 us
    pallas_call x3, Pallas kernels, expand(): pl.pallas_call(expand_kernel, grid=(rows // tile,), in_specs=[pl.BlockSpe...  15.5 us
  transfers between devices with their start and end apart: 23, of which 12 were waited for; matrix products, arithmetic and copies ran while one was open for 25% of the time, Pallas kernels for 8%

profile of v1, /device:TPU:0, one launch (start us, length us, event | category | flops | bytes accessed | tf_op | source)
XLA Modules:
  0.0 433.2 jit_solution(13920596362918319450)
XLA Ops:
  10.2 6.1 %reshape.121 = bf16[192,4,4,2,256]{4,3,2,1,0:T(2,128)(2,1)} reshape(bf16[192,8192]{1,0:T(8,128)(2,1)} %param.10) | data formatting | bytes 6291456 | tf_op jit(solution)/shard_map/reshape | solution.py:139
  16.3 10.2 %gather_fusion.5 = bf16[4,192,4,2,256]{4,3,2,1,0:T(2,128)(2,1)S(1)} fusion(bf16[192,4,4,2,256]{4,3,2,1,0:T(2,128)(2,1)} %reshape.121, s32[1024]{0:T(1024)S(1)} %pad_clamp_fusion), kind=kCustom, calls=%fused_computation.5 | custom fusion | bytes 6291472 | tf_op jit(solution)/shard_map/gather | solution.py:140
  44.3 37.2 %collective-permute-done.rest_1_ = bf16[16,192,256]{2,1,0:T(8,128)(2,1)} collective-permute-done((bf16[16,192,256]{2,1,0:T(8,128)(2,1)S(1)}, bf16[16,192,256]{2,1,0:T(8,128)(2,1)}, u32[]{:S(2)}, u32[]{:S(2)}) %collective-permute-start) | collective-permute-done | bytes 1572896 | tf_op jit(solution)/shard_map/ppermute | solution.py:122
  81.8 6.1 %reshape.111 = bf16[192,4,4,2,256]{4,3,2,1,0:T(2,128)(2,1)} reshape(bf16[192,8192]{1,0:T(8,128)(2,1)} %param.9) | data formatting | bytes 6291456 | tf_op jit(solution)/shard_map/reshape | solution.py:139
  87.9 10.0 %gather_fusion.1 = bf16[4,192,4,2,256]{4,3,2,1,0:T(2,128)(2,1)} fusion(bf16[192,4,4,2,256]{4,3,2,1,0:T(2,128)(2,1)} %reshape.111, s32[1024]{0:T(1024)S(1)} %pad_clamp_fusion), kind=kCustom, calls=%fused_computation.1 | custom fusion | bytes 6291472 | tf_op jit(solution)/shard_map/gather | solution.py:140
  123.4 8.8 %collective-permute-done.9.rest_1_ = bf16[16,64,256]{2,1,0:T(8,128)(2,1)} collective-permute-done((bf16[16,64,256]{2,1,0:T(8,128)(2,1)S(1)}, bf16[16,64,256]{2,1,0:T(8,128)(2,1)}, u32[]{:S(2)}, u32[]{:S(2)}) %collective-permute-start.9) | collective-permute-done | bytes 524320 | tf_op jit(solution)/shard_map/ppermute | solution.py:122
  132.2 44.9 %collective-permute-done.12.rest_1_ = bf16[16,64,256]{2,1,0:T(8,128)(2,1)} collective-permute-done((bf16[16,64,256]{2,1,0:T(8,128)(2,1)S(1)}, bf16[16,64,256]{2,1,0:T(8,128)(2,1)}, u32[]{:S(2)}, u32[]{:S(2)}) %collective-permute-start.12) | collective-permute-done | bytes 524320 | tf_op jit(solution)/shard_map/ppermute | solution.py:122
  177.1 11.2 %collective-permute-done.10.rest_2_ = bf16[16,64,256]{2,1,0:T(8,128)(2,1)} collective-permute-done((bf16[16,64,256]{2,1,0:T(8,128)(2,1)}, bf16[16,64,256]{2,1,0:T(8,128)(2,1)}, u32[]{:S(2)}, u32[]{:S(2)}) %collective-permute-start.10) | collective-permute-done | bytes 524320 | tf_op jit(solution)/shard_map/ppermute | solution.py:122
  189.0 10.6 %collective-permute-done.13.rest_2_ = bf16[16,64,256]{2,1,0:T(8,128)(2,1)} collective-permute-done((bf16[16,64,256]{2,1,0:T(8,128)(2,1)}, bf16[16,64,256]{2,1,0:T(8,128)(2,1)}, u32[]{:S(2)}, u32[]{:S(2)}) %collective-permute-start.13) | collective-permute-done | bytes 524320 | tf_op jit(solution)/shard_map/ppermute | solution.py:122
  199.6 11.2 %collective-permute-done.11.rest_3_ = bf16[16,64,256]{2,1,0:T(8,128)(2,1)} collective-permute-done((bf16[16,64,256]{2,1,0:T(8,128)(2,1)}, bf16[16,64,256]{2,1,0:T(8,128)(2,1)}, u32[]{:S(2)}, u32[]{:S(2)}) %collective-permute-start.11) | collective-permute-done | bytes 524320 | tf_op jit(solution)/shard_map/ppermute | solution.py:122
  210.8 6.3 %shrink.3 = bf16[1536,64]{1,0:T(8,128)(2,1)S(1)} custom-call(s32[1536,1]{1,0:T(8,128)S(1)} %reshape.193.ids_ref, bf16[1536,1024]{1,0:T(8,128)(2,1)} %bitcast.19.tokens_ref, bf16[16,64,256]{2,1,0:T(8,128)(2,1)S(1)} %constant_dynamic-slice_fusion.4.rest_0_, bf16[16,64,256]{2,1,0:T(8,128)(2,1)} %collective-permute-done.9.rest_1_, ...), custom_call_target="tpu_custom_call" | custom-call | flops 3221225472 | bytes 5242880 | tf_op jit(solution)/shard_map/shrink/pallas_call | solution.py:56
  222.1 14.7 %shrink.2 = bf16[1536,192]{1,0:T(8,128)(2,1)} custom-call(s32[1536,1]{1,0:T(8,128)S(1)} %reshape.193.ids_ref, bf16[1536,1024]{1,0:T(8,128)(2,1)} %bitcast.2.tokens_ref, bf16[16,192,256]{2,1,0:T(8,128)(2,1)S(1)} %constant_dynamic-slice_fusion.1.rest_0_, bf16[16,192,256]{2,1,0:T(8,128)(2,1)} %collective-permute-done.rest_1_, ...), custom_call_target="tpu_custom_call" | custom-call | flops 9663676416 | bytes 9437184 | tf_op jit(solution)/shard_map/shrink/pallas_call | solution.py:56
  236.8 15.6 %all-to-all-start.2 = ((bf16[8,192,192]{2,1,0:T(8,128)(2,1)}), bf16[8,192,192]{2,1,0:T(8,128)(2,1)}, u32[]{:S(2)}, u32[]{:S(2)}) async-start(bf16[8,192,192]{2,1,0:T(8,128)(2,1)} %bitcast.3), calls=%async_computation.2 | async-start | bytes 1572864 | tf_op jit(solution)/shard_map/all_to_all | solution.py:115
  252.5 16.1 %all-gather = bf16[8,192,64]{1,2,0:T(8,128)(2,1)S(1)} all-gather(bf16[1,192,64]{1,2,0:T(8,128)(2,1)S(1)} %bitcast.55), channel_id=1, replica_groups=mesh['groups'=2,'h'=4,'r'=4] {'groups','r'}, dimensions={0}, use_global_device_ids=true | all-gather | bytes 221184 | tf_op jit(solution)/shard_map/all_gather | solution.py:198
  268.8 6.5 %expand.5 = bf16[1536,1024]{1,0:T(8,128)(2,1)} custom-call(s32[1536,1]{1,0:T(8,128)S(1)} %reshape.193.ids_ref, bf16[1536,64]{1,0:T(8,128)(2,1)S(1)} %bitcast.39, bf16[16,64,256]{2,1,0:T(8,128)(2,1)S(1)} %copy-done.3, bf16[16,64,256]{2,1,0:T(8,128)(2,1)} %collective-permute-done.12.rest_1_, bf16[16,64,256]{2,1,0:T(8,128)(2,1)} %collective-permute-done.13.rest_2_, ...), custom_call_target="tpu_custom_call" | custom-call | flops 3221225472 | bytes 5242880 | tf_op jit(solution)/shard_map/expand/pallas_call | solution.py:94
  280.0 15.9 %collective-permute-done.3.rest_1_ = bf16[16,64,256]{2,1,0:T(8,128)(2,1)S(1)} collective-permute-done((bf16[16,64,256]{2,1,0:T(8,128)(2,1)S(1)}, bf16[16,64,256]{2,1,0:T(8,128)(2,1)S(1)}, u32[]{:S(2)}, u32[]{:S(2)}) %collective-permute-start.3) | collective-permute-done | bytes 524320 | tf_op jit(solution)/shard_map/ppermute | solution.py:122
  296.3 20.4 %collective-permute-done.6 = bf16[16,64,64]{2,1,0:T(8,128)(2,1)S(1)} collective-permute-done((bf16[16,64,64]{2,1,0:T(8,128)(2,1)S(1)}, bf16[16,64,64]{2,1,0:T(8,128)(2,1)S(1)}, u32[]{:S(2)}, u32[]{:S(2)}) %collective-permute-start.6) | collective-permute-done | bytes 131104 | tf_op jit(solution)/shard_map/ppermute | solution.py:122
  316.7 8.6 %collective-permute-done.7 = bf16[16,64,64]{2,1,0:T(8,128)(2,1)S(1)} collective-permute-done((bf16[16,64,64]{2,1,0:T(8,128)(2,1)S(1)}, bf16[16,64,64]{2,1,0:T(8,128)(2,1)S(1)}, u32[]{:S(2)}, u32[]{:S(2)}) %collective-permute-start.7) | collective-permute-done | bytes 131104 | tf_op jit(solution)/shard_map/ppermute | solution.py:122
  325.3 8.3 %collective-permute-done.8 = bf16[16,64,64]{2,1,0:T(8,128)(2,1)} collective-permute-done((bf16[16,64,64]{2,1,0:T(8,128)(2,1)S(1)}, bf16[16,64,64]{2,1,0:T(8,128)(2,1)}, u32[]{:S(2)}, u32[]{:S(2)}) %collective-permute-start.8) | collective-permute-done | bytes 131104 | tf_op jit(solution)/shard_map/ppermute | solution.py:122
  336.2 10.2 %all_gather.6 = bf16[1536,192]{1,0:T(8,128)(2,1)S(1)} all-gather(bf16[192,192]{1,0:T(8,128)(2,1)S(1)} %reduce_sum.24), channel_id=1, replica_groups=mesh['groups'=2,'h'=4,'r'=4] {'groups','r'}, dimensions={0}, use_global_device_ids=true | all-gather | bytes 663552 | tf_op jit(solution)/shard_map/all_gather | solution.py:198
  352.9 6.3 %expand.3 = bf16[1536,1024]{1,0:T(8,128)(2,1)} custom-call(s32[1536,1]{1,0:T(8,128)S(1)} %reshape.193.ids_ref, bf16[1536,64]{1,0:T(8,128)(2,1)S(1)} %get-tuple-element.21.low_ref, bf16[16,64,256]{2,1,0:T(8,128)(2,1)S(1)} %copy-done.1, bf16[16,64,256]{2,1,0:T(8,128)(2,1)S(1)} %collective-permute-done.3.rest_1_, ...), custom_call_target="tpu_custom_call" | custom-call | flops 3221225472 | bytes 5242880 | tf_op jit(solution)/shard_map/expand/pallas_call | solution.py:94
  369.0 6.2 %reshape.126 = bf16[2,4,192,4,256]{4,3,2,1,0:T(4,128)(2,1)} reshape(bf16[8,192,1024]{2,1,0:T(8,128)(2,1)} %all-to-all-done.7) | data formatting | bytes 6291456 | tf_op jit(solution)/shard_map/reshape | solution.py:147
  383.5 6.8 %copy.66 = bf16[192,4,4,2,256]{4,3,2,1,0:T(2,128)(2,1)} copy(bf16[192,4,4,2,256]{4,0,3,2,1:T(8,128)(2,1)} %bitcast.46) | data formatting | bytes 6291456 | tf_op jit(solution)/shard_map/gather | solution.py:148
  390.3 6.1 %reshape.127 = bf16[192,8192]{1,0:T(8,128)(2,1)} reshape(bf16[192,4,4,2,256]{4,3,2,1,0:T(2,128)(2,1)} %copy.66) | data formatting | bytes 6291456 | tf_op jit(solution)/shard_map/reshape | solution.py:149
  (88 shorter events, 127.8 us)
Async XLA Ops:
  0.6 295.3 %copy-start = (bf16[16,128,64]{1,2,0:T(8,128)(2,1)S(1)}, bf16[16,128,64]{1,2,0:T(8,128)(2,1)}, u32[]{:S(2)}) copy-start(bf16[16,128,64]{1,2,0:T(8,128)(2,1)} %param.16) | copy-start | bytes 786436
  5.0 31.7 %all-to-all-start = ((s32[8,1,192]{2,1,0:T(1,128)}), s32[8,1,192]{2,1,0:T(1,128)S(1)}, u32[]{:S(2)}, u32[]{:S(2)}) async-start(s32[8,1,192]{2,1,0:T(1,128)} %broadcast_in_dim.7), calls=%async_computation | async-start | bytes 16384 | tf_op jit(solution)/shard_map/all_to_all | solution.py:115
  36.7 73.2 %all-to-all-start.5 = ((bf16[8,192,1024]{2,1,0:T(8,128)(2,1)}), bf16[8,192,1024]{2,1,0:T(8,128)(2,1)}, u32[]{:S(2)}, u32[]{:S(2)}) async-start(bf16[8,192,1024]{2,1,0:T(8,128)(2,1)} %reshape.122), calls=%async_computation.5 | async-start | bytes 6291456 | tf_op jit(solution)/shard_map/all_to_all | solution.py:115
  42.7 38.8 %collective-permute-start = (bf16[16,192,256]{2,1,0:T(8,128)(2,1)S(1)}, bf16[16,192,256]{2,1,0:T(8,128)(2,1)}, u32[]{:S(2)}, u32[]{:S(2)}) collective-permute-start(bf16[16,192,256]{2,1,0:T(8,128)(2,1)S(1)} %constant_dynamic-slice_fusion.1.rest_0_), channel_id=1, source_target_pairs={{0,4},{4,8},{8,12},{12,0},{1,5},{5,9},{9,13},{13,1},{2,6},{6,10},{... | collective-permute-start | bytes 4718600 | tf_op jit(solution)/shard_map/ppermute | solution.py:122
  81.5 38.4 %collective-permute-start.1 = (bf16[16,192,256]{2,1,0:T(8,128)(2,1)}, bf16[16,192,256]{2,1,0:T(8,128)(2,1)}, u32[]{:S(2)}, u32[]{:S(2)}) collective-permute-start(bf16[16,192,256]{2,1,0:T(8,128)(2,1)} %collective-permute-done.rest_1_), channel_id=1, source_target_pairs={{0,4},{4,8},{8,12},{12,0},{1,5},{5,9},{9,13},{13,1},{2,6},{6,10},{... | collective-permute-start | bytes 4718600 | tf_op jit(solution)/shard_map/ppermute | solution.py:122
  109.9 108.0 %all-to-all-start.1 = ((bf16[8,192,1024]{2,1,0:T(8,128)(2,1)}), bf16[8,192,1024]{2,1,0:T(8,128)(2,1)}, u32[]{:S(2)}, u32[]{:S(2)}) async-start(bf16[8,192,1024]{2,1,0:T(8,128)(2,1)} %reshape.112), calls=%async_computation.1 | async-start | bytes 6291456 | tf_op jit(solution)/shard_map/all_to_all | solution.py:115
  115.5 16.7 %collective-permute-start.9 = (bf16[16,64,256]{2,1,0:T(8,128)(2,1)S(1)}, bf16[16,64,256]{2,1,0:T(8,128)(2,1)}, u32[]{:S(2)}, u32[]{:S(2)}) collective-permute-start(bf16[16,64,256]{2,1,0:T(8,128)(2,1)S(1)} %constant_dynamic-slice_fusion.4.rest_0_), channel_id=1, source_target_pairs={{0,4},{4,8},{8,12},{12,0},{1,5},{5,9},{9,13},{13,1},{2,6},{6,10},{... | collective-permute-start | bytes 1572872 | tf_op jit(solution)/shard_map/ppermute | solution.py:122
  119.9 102.2 %collective-permute-start.2 = (bf16[16,192,256]{2,1,0:T(8,128)(2,1)}, bf16[16,192,256]{2,1,0:T(8,128)(2,1)}, u32[]{:S(2)}, u32[]{:S(2)}) collective-permute-start(bf16[16,192,256]{2,1,0:T(8,128)(2,1)} %collective-permute-done.1.rest_2_), channel_id=1, source_target_pairs={{0,4},{4,8},{8,12},{12,0},{1,5},{5,9},{9,13},{13,1},{2,6},{6,10},{... | collective-permute-start | bytes 4718600 | tf_op jit(solution)/shard_map/ppermute | solution.py:122
  122.0 55.1 %collective-permute-start.12 = (bf16[16,64,256]{2,1,0:T(8,128)(2,1)S(1)}, bf16[16,64,256]{2,1,0:T(8,128)(2,1)}, u32[]{:S(2)}, u32[]{:S(2)}) collective-permute-start(bf16[16,64,256]{2,1,0:T(8,128)(2,1)S(1)} %get-tuple-element.16.rest_0_), channel_id=1, source_target_pairs={{0,4},{4,8},{8,12},{12,0},{1,5},{5,9},{9,13},{13,1},{2,6},{6,10},{... | collective-permute-start | bytes 1572872 | tf_op jit(solution)/shard_map/ppermute | solution.py:122
  132.2 56.2 %collective-permute-start.10 = (bf16[16,64,256]{2,1,0:T(8,128)(2,1)}, bf16[16,64,256]{2,1,0:T(8,128)(2,1)}, u32[]{:S(2)}, u32[]{:S(2)}) collective-permute-start(bf16[16,64,256]{2,1,0:T(8,128)(2,1)} %collective-permute-done.9.rest_1_), channel_id=1, source_target_pairs={{0,4},{4,8},{8,12},{12,0},{1,5},{5,9},{9,13},{13,1},{2,6},{6,10},{... | collective-permute-start | bytes 1572872 | tf_op jit(solution)/shard_map/ppermute | solution.py:122
  177.1 22.5 %collective-permute-start.13 = (bf16[16,64,256]{2,1,0:T(8,128)(2,1)}, bf16[16,64,256]{2,1,0:T(8,128)(2,1)}, u32[]{:S(2)}, u32[]{:S(2)}) collective-permute-start(bf16[16,64,256]{2,1,0:T(8,128)(2,1)} %collective-permute-done.12.rest_1_), channel_id=1, source_target_pairs={{0,4},{4,8},{8,12},{12,0},{1,5},{5,9},{9,13},{13,1},{2,6},{6,10},{... | collective-permute-start | bytes 1572872 | tf_op jit(solution)/shard_map/ppermute | solution.py:122
  188.3 22.5 %collective-permute-start.11 = (bf16[16,64,256]{2,1,0:T(8,128)(2,1)}, bf16[16,64,256]{2,1,0:T(8,128)(2,1)}, u32[]{:S(2)}, u32[]{:S(2)}) collective-permute-start(bf16[16,64,256]{2,1,0:T(8,128)(2,1)} %collective-permute-done.10.rest_2_), channel_id=1, source_target_pairs={{0,4},{4,8},{8,12},{12,0},{1,5},{5,9},{9,13},{13,1},{2,6},{6,10},{... | collective-permute-start | bytes 1572872 | tf_op jit(solution)/shard_map/ppermute | solution.py:122
  199.6 69.2 %collective-permute-start.14 = (bf16[16,64,256]{2,1,0:T(8,128)(2,1)}, bf16[16,64,256]{2,1,0:T(8,128)(2,1)}, u32[]{:S(2)}, u32[]{:S(2)}) collective-permute-start(bf16[16,64,256]{2,1,0:T(8,128)(2,1)} %collective-permute-done.13.rest_2_), channel_id=1, source_target_pairs={{0,4},{4,8},{8,12},{12,0},{1,5},{5,9},{9,13},{13,1},{2,6},{6,10},{... | collective-permute-start | bytes 1572872 | tf_op jit(solution)/shard_map/ppermute | solution.py:122
  218.0 18.8 %all-to-all-start.6 = ((bf16[8,192,64]{1,2,0:T(8,128)(2,1)}), bf16[8,192,64]{1,2,0:T(8,128)(2,1)S(1)}, u32[]{:S(2)}, u32[]{:S(2)}) async-start(bf16[8,192,64]{1,2,0:T(8,128)(2,1)} %copy.62), calls=%async_computation.6 | async-start | bytes 524288 | tf_op jit(solution)/shard_map/all_to_all | solution.py:115
  236.8 38.6 %all-to-all-start.2 = ((bf16[8,192,192]{2,1,0:T(8,128)(2,1)}), bf16[8,192,192]{2,1,0:T(8,128)(2,1)}, u32[]{:S(2)}, u32[]{:S(2)}) async-start(bf16[8,192,192]{2,1,0:T(8,128)(2,1)} %bitcast.3), calls=%async_computation.2 | async-start | bytes 1572864 | tf_op jit(solution)/shard_map/all_to_all | solution.py:115
  275.4 73.9 %all-to-all-start.7 = ((bf16[8,192,1024]{2,1,0:T(8,128)(2,1)}), bf16[8,192,1024]{2,1,0:T(8,128)(2,1)}, u32[]{:S(2)}, u32[]{:S(2)}) async-start(bf16[8,192,1024]{2,1,0:T(8,128)(2,1)} %bitcast.51), calls=%async_computation.7 | async-start | bytes 6291456 | tf_op jit(solution)/shard_map/all_to_all | solution.py:115
  280.0 16.0 %collective-permute-start.3 = (bf16[16,64,256]{2,1,0:T(8,128)(2,1)S(1)}, bf16[16,64,256]{2,1,0:T(8,128)(2,1)S(1)}, u32[]{:S(2)}, u32[]{:S(2)}) collective-permute-start(bf16[16,64,256]{2,1,0:T(8,128)(2,1)S(1)} %copy-done.1), channel_id=1, source_target_pairs={{0,4},{4,8},{8,12},{12,0},{1,5},{5,9},{9,13},{13,1},{2,6},{6,10},{... | collective-permute-start | bytes 1572872 | tf_op jit(solution)/shard_map/ppermute | solution.py:122
  296.0 39.0 %collective-permute-start.4 = (bf16[16,64,256]{2,1,0:T(8,128)(2,1)S(1)}, bf16[16,64,256]{2,1,0:T(8,128)(2,1)}, u32[]{:S(2)}, u32[]{:S(2)}) collective-permute-start(bf16[16,64,256]{2,1,0:T(8,128)(2,1)S(1)} %collective-permute-done.3.rest_1_), channel_id=1, source_target_pairs={{0,4},{4,8},{8,12},{12,0},{1,5},{5,9},{9,13},{13,1},{2,6},{6,10},{... | collective-permute-start | bytes 1572872 | tf_op jit(solution)/shard_map/ppermute | solution.py:122
  296.3 20.4 %collective-permute-start.6 = (bf16[16,64,64]{2,1,0:T(8,128)(2,1)S(1)}, bf16[16,64,64]{2,1,0:T(8,128)(2,1)S(1)}, u32[]{:S(2)}, u32[]{:S(2)}) collective-permute-start(bf16[16,64,64]{2,1,0:T(8,128)(2,1)S(1)} %copy.69), channel_id=1, source_target_pairs={{0,4},{4,8},{8,12},{12,0},{1,5},{5,9},{9,13},{13,1},{2,6},{6,10},{... | collective-permute-start | bytes 393224 | tf_op jit(solution)/shard_map/ppermute | solution.py:122
  316.7 8.6 %collective-permute-start.7 = (bf16[16,64,64]{2,1,0:T(8,128)(2,1)S(1)}, bf16[16,64,64]{2,1,0:T(8,128)(2,1)S(1)}, u32[]{:S(2)}, u32[]{:S(2)}) collective-permute-start(bf16[16,64,64]{2,1,0:T(8,128)(2,1)S(1)} %collective-permute-done.6), channel_id=1, source_target_pairs={{0,4},{4,8},{8,12},{12,0},{1,5},{5,9},{9,13},{13,1},{2,6},{6,10},{... | collective-permute-start | bytes 393224 | tf_op jit(solution)/shard_map/ppermute | solution.py:122
  325.3 8.3 %collective-permute-start.8 = (bf16[16,64,64]{2,1,0:T(8,128)(2,1)S(1)}, bf16[16,64,64]{2,1,0:T(8,128)(2,1)}, u32[]{:S(2)}, u32[]{:S(2)}) collective-permute-start(bf16[16,64,64]{2,1,0:T(8,128)(2,1)S(1)} %collective-permute-done.7), channel_id=1, source_target_pairs={{0,4},{4,8},{8,12},{12,0},{1,5},{5,9},{9,13},{13,1},{2,6},{6,10},{... | collective-permute-start | bytes 393224 | tf_op jit(solution)/shard_map/ppermute | solution.py:122
  334.9 17.9 %collective-permute-start.5 = (bf16[16,64,256]{2,1,0:T(8,128)(2,1)}, bf16[16,64,256]{2,1,0:T(8,128)(2,1)}, u32[]{:S(2)}, u32[]{:S(2)}) collective-permute-start(bf16[16,64,256]{2,1,0:T(8,128)(2,1)} %collective-permute-done.4.rest_2_), channel_id=1, source_target_pairs={{0,4},{4,8},{8,12},{12,0},{1,5},{5,9},{9,13},{13,1},{2,6},{6,10},{... | collective-permute-start | bytes 1572872 | tf_op jit(solution)/shard_map/ppermute | solution.py:122
  349.3 15.1 %all-to-all-start.4 = ((bf16[8,192,256]{2,1,0:T(8,128)(2,1)}), bf16[8,192,256]{2,1,0:T(8,128)(2,1)S(1)}, u32[]{:S(2)}, u32[]{:S(2)}) async-start(bf16[8,192,256]{2,1,0:T(8,128)(2,1)} %bitcast.7), calls=%async_computation.4 | async-start | bytes 1572864 | tf_op jit(solution)/shard_map/all_to_all | solution.py:115
  365.3 49.8 %all-to-all-start.3 = ((bf16[8,192,1024]{2,1,0:T(8,128)(2,1)}), bf16[8,192,1024]{2,1,0:T(8,128)(2,1)S(1)}, u32[]{:S(2)}, u32[]{:S(2)}) async-start(bf16[8,192,1024]{2,1,0:T(8,128)(2,1)} %bitcast.52), calls=%async_computation.3 | async-start | bytes 6291456 | tf_op jit(solution)/shard_map/all_to_all | solution.py:115
  (4 other events, 53.0 us)

commit v2 on v1

v2 whole, which is shorter than its diff:
```python
import functools

import jax
import jax.numpy as jnp
from jax import lax
from jax.experimental import pallas as pl
from jax.experimental.pallas import tpu as pltpu
from jax.sharding import Mesh, PartitionSpec as P

LANES = 128
CHUNK = 48
SET = 8
RANK = 64
SCALE = 2.0
VMEM_LIMIT = 48 * 1024 * 1024
PLANE = ("groups", "r")
REQ = ("h", "r")


def call(kernel, name, out_shape, flops, traffic, **kwargs):
    return pl.pallas_call(
        kernel,
        out_shape=out_shape,
        compiler_params=pltpu.CompilerParams(vmem_limit_bytes=VMEM_LIMIT),
        cost_estimate=pl.CostEstimate(flops=flops, bytes_accessed=traffic, transcendentals=0),
        name=name,
        **kwargs,
    )


def bf16(*shape):
    return jax.ShapeDtypeStruct(shape, jnp.bfloat16)


def nt_dot(left, right):
    return lax.dot_general(
        left, right, (((1,), (1,)), ((), ())), preferred_element_type=jnp.float32
    )


def shrink_rows(ids, tokens, panel_of, adapters, ranks):
    pair_of = ids >> 1
    wide = jnp.zeros((ids.shape[0], 2 * ranks), jnp.float32)
    for first in range(0, adapters, 4):
        part = None
        for tokens_piece, panel in zip(tokens, panel_of(first)):
            term = nt_dot(tokens_piece, panel.reshape(4 * ranks, panel.shape[2]))
            part = term if part is None else part + term
        for j in range(2):
            at = 2 * j * ranks
            wide = jnp.where(pair_of == first // 2 + j, part[:, at : at + 2 * ranks], wide)
    return jnp.where((ids & 1) == 1, wide[:, ranks:], wide[:, :ranks])


def shrink_kernel(ranks, ids_ref, tokens_ref, panel_ref, out_ref):
    low = shrink_rows(
        ids_ref[...],
        [tokens_ref[...]],
        lambda first: [panel_ref[first : first + 4, :ranks]],
        panel_ref.shape[0],
        ranks,
    )
    out_ref[...] = low.astype(out_ref.dtype).reshape(out_ref.shape)


def shrink(ids, tokens, panels, ranks, inner, tok_rows):
    rows, columns = tokens.shape
    adapters, held, _ = panels.shape
    tile = inner * tok_rows
    return call(
        functools.partial(shrink_kernel, ranks),
        "shrink",
        bf16(inner, rows // tile, tok_rows, ranks),
        2 * rows * columns * ranks * adapters,
        2 * (rows + adapters * held) * columns,
        grid=(rows // tile,),
        in_specs=[
            pl.BlockSpec((tile, 1), lambda i: (i, 0)),
            pl.BlockSpec((tile, columns), lambda i: (i, 0)),
            pl.BlockSpec((adapters, held, columns), lambda i: (0, 0, 0)),
        ],
        out_specs=pl.BlockSpec((inner, 1, tok_rows, ranks), lambda i: (0, i, 0, 0)),
    )(ids, tokens, panels)


def shrink_parts_kernel(ids_ref, panel_ref, *refs):
    pieces, adapters, ranks, width = panel_ref.shape
    members = len(refs) // 2
    rows = refs[0].shape[0]
    for s in range(0, members, 2):
        both = jnp.concatenate([refs[s][...], refs[s + 1][...]], axis=0)
        low = shrink_rows(
            ids_ref[s * rows : (s + 2) * rows],
            [both[:, k * width : (k + 1) * width] for k in range(pieces)],
            lambda first: [panel_ref[k, first : first + 4] for k in range(pieces)],
            adapters,
            ranks,
        ).astype(jnp.bfloat16)
        refs[members + s][...] = low[:rows]
        refs[members + s + 1][...] = low[rows:]


def shrink_parts(ids, tokens, panels):
    members, (rows, columns) = len(tokens), tokens[0].shape
    pieces, adapters, ranks, width = panels.shape
    vmem = pl.BlockSpec(memory_space=pltpu.VMEM)
    return call(
        shrink_parts_kernel,
        "shrink_parts",
        [bf16(rows, ranks)] * members,
        2 * members * rows * columns * ranks * adapters,
        2 * (members * rows + adapters * ranks) * columns,
        in_specs=[vmem] * (2 + members),
        out_specs=[vmem] * members,
    )(ids, panels, *tokens)


def spread_rows(ids, low, adapters):
    spread = jnp.concatenate([low] * adapters, axis=1)
    lane_adapter = lax.broadcasted_iota(jnp.int32, spread.shape, 1) // low.shape[1]
    return jnp.where(lane_adapter == ids, spread, jnp.zeros_like(spread))


def expand_kernel(ids_ref, low_ref, panel_ref, out_ref):
    pieces, adapters, _, width = panel_ref.shape
    ranks = low_ref.shape[1]
    spread = spread_rows(ids_ref[...], low_ref[...], adapters)
    for k in range(pieces):
        panel = panel_ref[k, :, :ranks].reshape(adapters * ranks, width)
        full = jnp.dot(spread, panel, preferred_element_type=jnp.float32)
        out_ref[:, k * width : (k + 1) * width] = (SCALE * full).astype(out_ref.dtype)


def expand(ids, low, panels, tile):
    rows, ranks = low.shape
    pieces, adapters, _, width = panels.shape
    columns = width * pieces
    return call(
        expand_kernel,
        "expand",
        bf16(rows, columns),
        2 * rows * columns * ranks * adapters,
        2 * (rows + adapters * ranks) * columns,
        grid=(rows // tile,),
        in_specs=[
            pl.BlockSpec((tile, 1), lambda i: (i, 0)),
            pl.BlockSpec((tile, ranks), lambda i: (i, 0)),
            pl.BlockSpec(panels.shape, lambda i: (0, 0, 0, 0)),
        ],
        out_specs=pl.BlockSpec((tile, columns), lambda i: (i, 0)),
    )(ids, low, panels)


def expand_joint_kernel(g_ref, ids_ref, low_ref, panel_ref, out_ref):
    pieces, adapters, folded, width = panel_ref.shape
    ranks = low_ref.shape[1] // 3
    rows = folded - ranks
    narrow = rows * width // ranks
    ids = ids_ref[...]
    spread = spread_rows(ids, low_ref[:, :ranks], adapters)
    for k in range(pieces):
        panel = panel_ref[k, :, :ranks].reshape(adapters * ranks, width)
        full = jnp.dot(spread, panel, preferred_element_type=jnp.float32)
        out_ref[:, k * width : (k + 1) * width] = (SCALE * full).astype(out_ref.dtype)
    low_kv = jnp.where(g_ref[0] == 0, low_ref[:, ranks : 2 * ranks], low_ref[:, 2 * ranks :])
    spread = spread_rows(ids, low_kv, adapters)
    wide = []
    for k in range(pieces):
        parts = [
            panel_ref[k, :, ranks:, j * narrow : (j + 1) * narrow]
            for j in range(ranks // rows)
        ]
        wide.append(jnp.concatenate(parts, axis=1))
    panel = jnp.concatenate(wide, axis=2).reshape(adapters * ranks, pieces * narrow)
    full = jnp.dot(spread, panel, preferred_element_type=jnp.float32)
    out_ref[:, pieces * width :] = (SCALE * full).astype(out_ref.dtype)


def expand_joint(g, ids, low, panels, tile):
    rows, ranks = low.shape[0], low.shape[1] // 3
    pieces, adapters, folded, width = panels.shape
    columns = pieces * (width + (folded - ranks) * width // ranks)
    return call(
        expand_joint_kernel,
        "expand_joint",
        bf16(rows, columns),
        2 * rows * columns * ranks * adapters,
        2 * (rows + adapters * ranks) * columns,
        grid=(rows // tile,),
        in_specs=[
            pl.BlockSpec(memory_space=pltpu.SMEM),
            pl.BlockSpec((tile, 1), lambda i: (i, 0)),
            pl.BlockSpec((tile, 3 * ranks), lambda i: (i, 0)),
            pl.BlockSpec(panels.shape, lambda i: (0, 0, 0, 0)),
        ],
        out_specs=pl.BlockSpec((tile, columns), lambda i: (i, 0)),
    )(g, ids, low, panels)


def expand_parts_kernel(p_ref, ids_ref, low_ref, panel_ref, *out_refs):
    pieces, adapters, ranks, width = panel_ref.shape
    rows = low_ref.shape[1]
    for s in range(0, len(out_refs), 2):
        pair = [low_ref[p_ref[0] ^ s], low_ref[p_ref[0] ^ (s + 1)]]
        spread = spread_rows(
            ids_ref[s * rows : (s + 2) * rows], jnp.concatenate(pair, axis=0), adapters
        )
        for k in range(pieces):
            panel = panel_ref[k].reshape(adapters * ranks, width)
            full = jnp.dot(spread, panel, preferred_element_type=jnp.float32)
            full = (SCALE * full).astype(jnp.bfloat16)
            out_refs[s][:, k * width : (k + 1) * width] = full[:rows]
            out_refs[s + 1][:, k * width : (k + 1) * width] = full[rows:]


def expand_parts(p, ids, low, panels):
    members, rows, ranks = low.shape
    pieces, adapters, _, width = panels.shape
    columns = pieces * width
    vmem = pl.BlockSpec(memory_space=pltpu.VMEM)
    return call(
        expand_parts_kernel,
        "expand_parts",
        [bf16(rows, columns)] * members,
        2 * members * rows * columns * ranks * adapters,
        2 * (members * rows + adapters * ranks) * columns,
        in_specs=[pl.BlockSpec(memory_space=pltpu.SMEM)] + [vmem] * 3,
        out_specs=[vmem] * members,
    )(p, ids, low, panels)


def exchange(array, axes):
    return lax.all_to_all(array, axes, split_axis=0, concat_axis=0, tiled=True)


def swap_parts(parts):
    members = len(parts)
    return [parts[0]] + [
        lax.ppermute(parts[s], PLANE, [(d, d ^ s) for d in range(members)])
        for s in range(1, members)
    ]


def along_h(array):
    pieces = lax.all_gather(array, "h", axis=0)
    if array.shape[2] % LANES == 0:
        return pieces
    return pieces.transpose(1, 2, 0, 3).reshape((1,) + array.shape[:2] + (-1,))


def piece_places(member, count, inner, groups):
    g, r = member // inner, member % inner
    return [(k * inner + r) * groups + g for k in range(count)]


def window(place, width):
    start = place * width
    return pl.ds(start if isinstance(start, int) else pl.multiple_of(start, width), width)


def pack_parts_kernel(count, inner, groups, p_ref, source_ref, *out_refs):
    width = out_refs[0].shape[1] // count
    for s, out_ref in enumerate(out_refs):
        places = piece_places(p_ref[0] ^ s, count, inner, groups)
        for k, place in enumerate(places):
            out_ref[:, k * width : (k + 1) * width] = source_ref[:, window(place, width)]


def pack_parts(array, p, count, inner, groups):
    rows, columns = array.shape
    members = groups * inner
    width = columns // (count * members)
    if width % LANES:
        cut = array.reshape(rows, count, inner, groups, width).transpose(3, 2, 0, 1, 4)
        cut = cut.reshape(members, rows, count * width)
        return [lax.dynamic_index_in_dim(cut, p[0] ^ s, keepdims=False) for s in range(members)]
    return call(
        functools.partial(pack_parts_kernel, count, inner, groups),
        "pack_parts",
        [bf16(rows, count * width)] * members,
        0,
        4 * rows * columns,
        grid_spec=pltpu.PrefetchScalarGridSpec(
            num_scalar_prefetch=1,
            grid=(rows // CHUNK,),
            in_specs=[pl.BlockSpec((CHUNK, columns), lambda i, p_ref: (i, 0))],
            out_specs=[pl.BlockSpec((CHUNK, count * width), lambda i, p_ref: (i, 0))] * members,
        ),
    )(p, array)


def unpack_parts_kernel(count, inner, groups, p_ref, *refs):
    out_ref = refs[-1]
    width = refs[0].shape[1] // count
    for s, part_ref in enumerate(refs[:-1]):
        places = piece_places(p_ref[0] ^ s, count, inner, groups)
        for k, place in enumerate(places):
            out_ref[:, window(place, width)] = part_ref[:, k * width : (k + 1) * width]


def unpack_parts(parts, p, count, inner, groups):
    members, (rows, columns) = len(parts), parts[0].shape
    if (columns // count) % LANES:
        stacked = jnp.stack(parts)[p[0] ^ jnp.arange(members)]
        return unpack(stacked, count, inner, groups)
    return call(
        functools.partial(unpack_parts_kernel, count, inner, groups),
        "unpack_parts",
        bf16(rows, columns * members),
        0,
        4 * rows * columns * members,
        grid_spec=pltpu.PrefetchScalarGridSpec(
            num_scalar_prefetch=1,
            grid=(rows // CHUNK,),
            in_specs=[pl.BlockSpec((CHUNK, columns), lambda i, p_ref: (i, 0))] * members,
            out_specs=pl.BlockSpec((CHUNK, columns * members), lambda i, p_ref: (i, 0)),
        ),
    )(p, *parts)


def unpack_kernel(count, inner, groups, source_ref, out_ref):
    members, _, columns = source_ref.shape
    width = columns // count
    for m in range(members):
        for k, place in enumerate(piece_places(m, count, inner, groups)):
            out_ref[:, window(place, width)] = source_ref[m, :, k * width : (k + 1) * width]


def unpack(array, count, inner, groups):
    members, rows, columns = array.shape
    width = columns // count
    shape = (rows, columns * members)
    if width % LANES:
        cut = array.reshape(groups, inner, rows, count, width).transpose(2, 3, 1, 0, 4)
        return cut.reshape(shape)
    return call(
        functools.partial(unpack_kernel, count, inner, groups),
        "unpack",
        bf16(*shape),
        0,
        4 * array.size,
        grid=(rows // CHUNK,),
        in_specs=[pl.BlockSpec((members, CHUNK, columns), lambda i: (0, i, 0))],
        out_specs=pl.BlockSpec((CHUNK, columns * members), lambda i: (i, 0)),
    )(array)


def pack_kernel(source_ref, out_ref):
    width = out_ref.shape[2]
    for m in range(out_ref.shape[0]):
        out_ref[m] = source_ref[:, m * width : (m + 1) * width]


def pack(array, members):
    rows, columns = array.shape
    width = columns // members
    return call(
        pack_kernel,
        "pack",
        bf16(members, rows, width),
        0,
        4 * array.size,
        grid=(rows // CHUNK,),
        in_specs=[pl.BlockSpec((CHUNK, columns), lambda i: (i, 0))],
        out_specs=pl.BlockSpec((members, CHUNK, width), lambda i: (0, i, 0)),
    )(array)


def unpack_joint_kernel(count, inner, groups, narrow, parts_ref, q_ref, k_ref, v_ref):
    members, _, columns = parts_ref.shape
    width = columns // count - narrow
    for m in range(members):
        for k, place in enumerate(piece_places(m, count, inner, groups)):
            q_ref[:, window(place, width)] = parts_ref[m, :, k * width : (k + 1) * width]
    for start, out_ref in ((0, k_ref), (inner, v_ref)):
        for h in range(count):
            for r in range(0, inner, 2):
                at = count * width + h * narrow
                pair = [parts_ref[start + r + j, :, at : at + narrow] for j in range(2)]
                at = (h * inner + r) * narrow
                out_ref[:, at : at + 2 * narrow] = jnp.concatenate(pair, axis=1)


def unpack_joint(parts, narrow, count, inner, groups):
    members, rows, columns = parts.shape
    q_columns = (columns - count * narrow) * members
    kv_columns = count * inner * narrow
    return call(
        functools.partial(unpack_joint_kernel, count, inner, groups, narrow),
        "unpack_joint",
        (bf16(rows, q_columns), bf16(rows, kv_columns), bf16(rows, kv_columns)),
        0,
        4 * parts.size,
        grid=(rows // CHUNK,),
        in_specs=[pl.BlockSpec((members, CHUNK, columns), lambda i: (0, i, 0))],
        out_specs=[
            pl.BlockSpec((CHUNK, q_columns), lambda i: (i, 0)),
            pl.BlockSpec((CHUNK, kv_columns), lambda i: (i, 0)),
            pl.BlockSpec((CHUNK, kv_columns), lambda i: (i, 0)),
        ],
    )(parts)


def shards(
    normed_hidden,
    attn_mixed,
    adapter_ids,
    send_slot,
    padded_row,
    fetch_list,
    shrink_panels,
    expand_qo,
    expand_kv,
):
    groups, count, inner = (lax.axis_size(a) for a in ("groups", "h", "r"))
    g, h, r = (lax.axis_index(a) for a in ("groups", "h", "r"))
    p = (g * inner + r).reshape(1)
    devices = count * inner
    members = groups * inner
    tok_rows = normed_hidden.shape[0]
    slot_rows = 2 * tok_rows // devices
    rows = members * tok_rows
    tile = 2 * tok_rows

    def own_columns(panel):
        width = panel.shape[2] // groups
        return lax.dynamic_slice_in_dim(panel, g * width, width, 2)

    own_q = own_columns(expand_qo[:, :RANK])
    fold = groups == 2 and own_q.shape[2] % LANES == 0
    if fold:
        own_kv = lax.dynamic_slice_in_dim(expand_kv, g * RANK, RANK, 1)
        folds = own_q.shape[2] // own_kv.shape[2]
        own_kv = jnp.concatenate(jnp.split(own_kv, folds, axis=1), axis=2)
        b_q = along_h(jnp.concatenate([own_q, own_kv], axis=1))
    else:
        b_q = along_h(own_q)
        b_kv = along_h(own_columns(expand_kv))

    a_o = along_h(own_columns(shrink_panels[:, 3 * RANK :]))

    listed = fetch_list[send_slot // slot_rows]
    keep = jnp.any(listed == adapter_ids[:, None], axis=1)
    own_ids = jnp.where(keep, adapter_ids, -1)
    group_ids = exchange(jnp.broadcast_to(own_ids, (devices, tok_rows)), REQ)
    near_ids = lax.dynamic_slice_in_dim(group_ids, h * inner, inner, 0)
    if groups == 2:
        far_ids = lax.ppermute(near_ids, "groups", [(0, 1), (1, 0)])
        first, second = jnp.where(g == 0, near_ids, far_ids), jnp.where(g == 0, far_ids, near_ids)
        plane_ids = jnp.concatenate([first, second], axis=0)
    else:
        plane_ids = lax.all_gather(near_ids, "groups", axis=0, tiled=True)
    swap_ids = plane_ids[p ^ jnp.arange(members)].reshape(rows, 1)
    plane_ids = plane_ids.reshape(rows, 1)
    group_ids = group_ids.reshape(devices * tok_rows, 1)

    packed_x = pack(normed_hidden, devices)
    sent_x = exchange(packed_x, REQ)
    attn_mixed, packed_x = lax.optimization_barrier((attn_mixed, packed_x))
    sent_y = swap_parts(pack_parts(attn_mixed, p, count, inner, groups))

    sent_x, sent_y, group_ids, swap_ids, plane_ids = lax.optimization_barrier(
        (sent_x, sent_y, group_ids, swap_ids, plane_ids)
    )
    tokens = sent_x.reshape(devices * tok_rows, -1)
    part = shrink(group_ids, tokens, shrink_panels, 3 * RANK, inner, tok_rows)
    part, a_o = lax.optimization_barrier((part, a_o))
    near = jnp.sum(exchange(part, "r").astype(jnp.float32), axis=0).astype(jnp.bfloat16)

    parts_o = swap_parts(shrink_parts(swap_ids, sent_y, a_o))
    low_o = sum(piece.astype(jnp.float32) for piece in parts_o).astype(jnp.bfloat16)
    near, low_o = lax.optimization_barrier((near, low_o))
    low_o = lax.all_gather(low_o, PLANE, axis=0)

    far = exchange(near, "h")
    far, low_o, own_o = lax.optimization_barrier((far, low_o, own_columns(expand_qo[:, RANK:])))
    b_o = along_h(own_o)
    low = jnp.sum(far.astype(jnp.float32), axis=0).astype(jnp.bfloat16)
    low = lax.all_gather(low, PLANE, axis=0, tiled=True)

    def home(low_part, panels):
        full = expand(plane_ids, low_part, panels, tile)
        return exchange(full.reshape(members, tok_rows, -1), PLANE)

    if fold:
        full = expand_joint(g.reshape(1), plane_ids, low, b_q, tile)
        full, low_o = lax.optimization_barrier((full, low_o))
        parts = exchange(full.reshape(members, tok_rows, -1), PLANE)
        narrow = expand_kv.shape[2]
        delta_q, delta_k, delta_v = unpack_joint(parts, narrow, count, inner, groups)
        full_o = expand_parts(p, swap_ids, low_o, b_o)
        delta_o = unpack_parts(swap_parts(full_o), p, count, inner, groups)
        return delta_q, delta_k, delta_v, delta_o
    full_o = expand_parts(p, swap_ids, low_o, b_o)
    delta_o = unpack_parts(swap_parts(full_o), p, count, inner, groups)
    low_k, low_v = low[:, RANK : 2 * RANK], low[:, 2 * RANK :]
    delta_k = unpack(home(low_k, b_kv[:, :, :RANK]), count, inner, groups)
    delta_v = unpack(home(low_v, b_kv[:, :, RANK:]), count, inner, groups)
    delta_q = unpack(home(low[:, :RANK], b_q), count, inner, groups)
    return delta_q, delta_k, delta_v, delta_o


def solution(mesh):
    groups, devices = mesh.devices.shape
    inner = max(SET // groups, 1)
    cut = Mesh(mesh.devices.reshape(groups, devices // inner, inner), ("groups", "h", "r"))
    by_token = P(("groups", "h", "r"))
    by_token_rows = P(("groups", "h", "r"), None)
    by_column = P(None, None, ("h", "r"))
    in_specs = (
        (by_token_rows,) * 2 + (by_token,) * 3 + (P("groups", None),) + (by_column,) * 3
    )
    out_specs = (by_token_rows,) * 4
    return jax.shard_map(shards, mesh=cut, in_specs=in_specs, out_specs=out_specs, check_vma=False)
```

time: 436 us -> 309 us (0.71)
  local copies, waits for them, and re-layouts: 129 us -> 14.3 us
  waiting for transfers between devices: 185 us -> 151 us
  between operations: 1.1 us -> 14 us
  Pallas kernels: 36.5 us -> 46.8 us
  blocking collectives: 26.3 us -> 19.8 us
  starting transfers between devices: 49.5 us -> 54.1 us
    ppermute x15 -> x22, waiting for transfers between devices: 180 us -> 92.7 us  [the longest x21 83.1 us: swap_parts(): lax.ppermute(parts[s], PLANE, [(d, d ^ s) for d in range(members)])]
    reshape x12 -> x3, local copies, waits for them, and re-layouts: 52.6 us -> 2.16 us  [the longest x1 1.4 us: shards(): group_ids = group_ids.reshape(devices * tok_rows, 1)]
    gather x8 -> x1, local copies, waits for them, and re-layouts: 43.7 us -> 0.68 us  [shards(): swap_ids = plane_ids[p ^ jnp.arange(members)].reshape(rows, 1)]
    all_to_all x8 -> x5, waiting for transfers between devices: 5.26 us -> 36.5 us  [exchange(): return lax.all_to_all(array, axes, split_axis=0, concat_axis=0, tiled=True)]
    all_gather x0 -> x3, waiting for transfers between devices: none -> 21.9 us  [along_h(): pieces = lax.all_gather(array, 'h', axis=0)]
    ppermute x15 -> x22, starting transfers between devices: 3.97 us -> 20.6 us  [the longest x21 20 us: swap_parts(): lax.ppermute(parts[s], PLANE, [(d, d ^ s) for d in range(members)])]
    all_to_all x8 -> x5, starting transfers between devices: 45.6 us -> 33.4 us  [exchange(): return lax.all_to_all(array, axes, split_axis=0, concat_axis=0, tiled=True)]
    pallas_call x5 -> x8, Pallas kernels: 36.5 us -> 46.8 us  [the longest x1 14.5 us: shrink(): call(functools.partial(shrink_kernel, ranks), 'shrink', bf16(inner, rows...]
  transfers between devices with their start and end apart: 23 -> 30, of which waited for: 12 -> 14; matrix products, arithmetic and copies ran while one was open for 25% -> 5% of each run, Pallas kernels for 8% -> 14%
where the time goes in v2:
time: 309 us; the launch traced here: 308 us
  waiting for transfers between devices  151 us (49%)
  starting transfers between devices  54.1 us (18%)
  Pallas kernels  46.8 us (15%)
  blocking collectives  19.8 us (6%)
  local copies, waits for them, and re-layouts  14.3 us (5%)
  between operations  14 us (5%)
  other arithmetic  7.83 us (3%)
    ppermute x21, waiting for transfers between devices, swap_parts(): lax.ppermute(parts[s], PLANE, [(d, d ^ s) for d in range(members)])  83.1 us
    all_to_all x5, waiting for transfers between devices, exchange(): return lax.all_to_all(array, axes, split_axis=0, concat_axis=0, tiled=True)  36.5 us
    all_to_all x5, starting transfers between devices, exchange(): return lax.all_to_all(array, axes, split_axis=0, concat_axis=0, tiled=True)  33.4 us
    all_gather x3, waiting for transfers between devices, along_h(): pieces = lax.all_gather(array, 'h', axis=0)  21.9 us
    ppermute x21, starting transfers between devices, swap_parts(): lax.ppermute(parts[s], PLANE, [(d, d ^ s) for d in range(members)])  20 us
    pallas_call x1, Pallas kernels, shrink(): call(functools.partial(shrink_kernel, ranks), 'shrink', bf16(inner, rows...  14.5 us
    all_gather x1, blocking collectives, shards(): low = lax.all_gather(low, PLANE, axis=0, tiled=True)  10.6 us
    ppermute x1, waiting for transfers between devices, shards(): far_ids = lax.ppermute(near_ids, 'groups', [(0, 1), (1, 0)])  9.52 us
  transfers between devices with their start and end apart: 30, of which 14 were waited for; matrix products, arithmetic and copies ran while one was open for 5% of the time, Pallas kernels for 14%

profile of v2, /device:TPU:0, one launch (start us, length us, event | category | flops | bytes accessed | tf_op | source)
XLA Modules:
  0.0 308.0 jit_solution(4796522217819648060)
XLA Ops:
  11.5 7.4 %all-to-all-start.1 = ((s32[16,1,192]{2,1,0:T(1,128)}), s32[16,1,192]{2,1,0:T(1,128)S(1)}, u32[]{:S(2)}, u32[]{:S(2)}) async-start(s32[16,1,192]{2,1,0:T(1,128)} %broadcast_in_dim.11), calls=%async_computation.1 | async-start | bytes 32768 | tf_op jit(solution)/shard_map/all_to_all | solution.py:233
  18.9 4.2 %pack.1 = bf16[16,192,512]{2,1,0:T(8,128)(2,1)} custom-call(bf16[192,8192]{1,0:T(8,128)(2,1)} %source_ref.1), custom_call_target="tpu_custom_call" | custom-call | bytes 6291456 | tf_op jit(solution)/shard_map/pack/pallas_call | solution.py:357
  25.4 4.5 %all-to-all-start = ((bf16[16,192,512]{2,1,0:T(8,128)(2,1)}), bf16[16,192,512]{2,1,0:T(8,128)(2,1)}, u32[]{:S(2)}, u32[]{:S(2)}) async-start(bf16[16,192,512]{2,1,0:T(8,128)(2,1)} %pack.1), calls=%async_computation | async-start | bytes 6291456 | tf_op jit(solution)/shard_map/all_to_all | solution.py:233
  35.8 3.9 %pack_parts.1 = (bf16[192,1024]{1,0:T(8,128)(2,1)S(1)}, bf16[192,1024]{1,0:T(8,128)(2,1)}, bf16[192,1024]{1,0:T(8,128)(2,1)}, bf16[192,1024]{1,0:T(8,128)(2,1)},...) custom-call(s32[1]{0:T(128)} %bitcast.1.p_ref, ...), custom_call_target="tpu_custom_call" | custom-call | bytes 6291456 | tf_op jit(solution)/shard_map/pack_parts/pallas_call | solution.py:277
  43.7 9.5 %collective-permute-done.7 = s32[4,192]{1,0:T(4,128)S(1)} collective-permute-done((s32[4,192]{1,0:T(4,128)S(1)}, s32[4,192]{1,0:T(4,128)S(1)}, u32[]{:S(2)}, u32[]{:S(2)}) %collective-permute-start.7) | collective-permute-done | bytes 3104 | tf_op jit(solution)/shard_map/ppermute | solution.py:448
  55.9 3.7 %collective-permute-done.1.refs_2_ = bf16[192,1024]{1,0:T(8,128)(2,1)S(1)} collective-permute-done((bf16[192,1024]{1,0:T(8,128)(2,1)}, bf16[192,1024]{1,0:T(8,128)(2,1)S(1)}, u32[]{:S(2)}, u32[]{:S(2)}) %collective-permute-start.1) | collective-permute-done | bytes 393248 | tf_op jit(solution)/shard_map/ppermute | solution.py:239
  64.3 27.0 %collective-permute-done.2.refs_3_ = bf16[192,1024]{1,0:T(8,128)(2,1)S(1)} collective-permute-done((bf16[192,1024]{1,0:T(8,128)(2,1)}, bf16[192,1024]{1,0:T(8,128)(2,1)S(1)}, u32[]{:S(2)}, u32[]{:S(2)}) %collective-permute-start.2) | collective-permute-done | bytes 393248 | tf_op jit(solution)/shard_map/ppermute | solution.py:239
  91.4 33.0 %all-to-all-done = bf16[16,192,512]{2,1,0:T(8,128)(2,1)} async-done(((bf16[16,192,512]{2,1,0:T(8,128)(2,1)}), bf16[16,192,512]{2,1,0:T(8,128)(2,1)}, u32[]{:S(2)}, u32[]{:S(2)}) %all-to-all-start) | async-done | bytes 3145760 | tf_op jit(solution)/shard_map/all_to_all | solution.py:233
  125.5 14.5 %shrink.1 = bf16[4,4,192,192]{3,2,1,0:T(8,128)(2,1)} custom-call(s32[3072,1]{1,0:T(8,128)S(1)} %copy.21.ids_ref, bf16[3072,512]{1,0:T(8,128)(2,1)} %bitcast.3.tokens_ref, bf16[16,256,512]{2,1,0:T(8,128)(2,1)} %panel_ref.1), custom_call_target="tpu_custom_call" | custom-call | flops 9663676416 | bytes 7340032 | tf_op jit(solution)/shard_map/shrink/pallas_call | solution.py:70
  140.0 6.4 %all-to-all-start.2 = ((bf16[4,4,192,192]{3,2,1,0:T(8,128)(2,1)}), bf16[4,4,192,192]{3,2,1,0:T(8,128)(2,1)}, u32[]{:S(2)}, u32[]{:S(2)}) async-start(bf16[4,4,192,192]{3,2,1,0:T(8,128)(2,1)} %shrink.1), calls=%async_computation.2 | async-start | bytes 3145728 | tf_op jit(solution)/shard_map/all_to_all | solution.py:233
  146.7 5.6 %shrink_parts.1 = (bf16[192,64]{1,0:T(8,128)(2,1)S(1)}, bf16[192,64]{1,0:T(8,128)(2,1)S(1)}, bf16[192,64]{1,0:T(8,128)(2,1)S(1)}, bf16[192,64]{1,0:T(8,128)(2,1)...) custom-call(s32[1536,1]{1,0:T(8,128)S(1)} %copy.22.ids_ref, ...), custom_call_target="tpu_custom_call" | custom-call | flops 3221225472 | bytes 5242880 | tf_op jit(solution)/shard_map/shrink_parts/pallas_call | solution.py:107
  152.3 4.1 %collective-permute-start.14 = (bf16[192,64]{1,0:T(8,128)(2,1)S(1)}, bf16[192,64]{1,0:T(8,128)(2,1)S(1)}, u32[]{:S(2)}, u32[]{:S(2)}) collective-permute-start(bf16[192,64]{1,0:T(8,128)(2,1)S(1)} %get-tuple-element.83), channel_id=1, source_target_pairs={{0,19},{1,18},{2,17},{3,16},{16,3},{17,2},{18,1},{19,0},{4,23},{5,... | collective-permute-start | bytes 73736 | tf_op jit(solution)/shard_map/ppermute | solution.py:239
  162.0 8.9 %collective-permute-done.10 = bf16[192,64]{1,0:T(8,128)(2,1)S(1)} collective-permute-done((bf16[192,64]{1,0:T(8,128)(2,1)S(1)}, bf16[192,64]{1,0:T(8,128)(2,1)S(1)}, u32[]{:S(2)}, u32[]{:S(2)}) %collective-permute-start.10) | collective-permute-done | bytes 24608 | tf_op jit(solution)/shard_map/ppermute | solution.py:239
  174.4 10.6 %all-to-all-start.3 = ((bf16[4,192,192]{2,1,0:T(8,128)(2,1)}), bf16[4,192,192]{2,1,0:T(8,128)(2,1)S(1)}, u32[]{:S(2)}, u32[]{:S(2)}) async-start(bf16[4,192,192]{2,1,0:T(8,128)(2,1)} %reduce_sum.24), calls=%async_computation.3 | async-start | bytes 786432 | tf_op jit(solution)/shard_map/all_to_all | solution.py:233
  186.0 9.3 %all-gather.4 = bf16[8,192,64]{1,2,0:T(8,128)(2,1)S(1)} all-gather(bf16[1,192,64]{1,2,0:T(8,128)(2,1)S(1)} %copy.23), channel_id=3, replica_groups=mesh['groups'=2,'h'=4,'r'=4] {'groups','r'}, dimensions={0}, use_global_device_ids=true | all-gather | bytes 221184 | tf_op jit(solution)/shard_map/all_gather | solution.py:473
  197.0 10.6 %all_gather.31.low_ref = bf16[1536,192]{1,0:T(8,128)(2,1)S(1)} all-gather(bf16[192,192]{1,0:T(8,128)(2,1)S(1)} %reduce_sum.25), channel_id=1, replica_groups=mesh['groups'=2,'h'=4,'r'=4] {'groups','r'}, dimensions={0}, use_global_device_ids=true | all-gather | bytes 663552 | tf_op jit(solution)/shard_map/all_gather | solution.py:479
  209.3 6.0 %expand_joint.1 = bf16[1536,1280]{1,0:T(8,128)(2,1)} custom-call(s32[1]{0:T(128)} %bitcast.g_ref, s32[1536,1]{1,0:T(8,128)S(1)} %copy.25.ids_ref, bf16[1536,192]{1,0:T(8,128)(2,1)S(1)} %all_gather.31.low_ref, bf16[4,16,80,256]{3,2,1,0:T(8,128)(2,1)S(1)} %bitcast.17), custom_call_target="tpu_custom_call" | custom-call | flops 4026531840 | bytes 6553600 | tf_op jit(solution)/shard_map/expand_joint/pallas_call | solution.py:183
  215.3 4.5 %all-to-all-start.4 = ((bf16[8,192,1280]{2,1,0:T(8,128)(2,1)}), bf16[8,192,1280]{2,1,0:T(8,128)(2,1)}, u32[]{:S(2)}, u32[]{:S(2)}) async-start(bf16[8,192,1280]{2,1,0:T(8,128)(2,1)} %bitcast.18), calls=%async_computation.4 | async-start | bytes 7864320 | tf_op jit(solution)/shard_map/all_to_all | solution.py:233
  220.0 21.9 %all-gather.13.cloned.1.call-done = bf16[64,64,256]{2,1,0:T(8,128)(2,1)} async-done(((bf16[16,64,256]{2,1,0:T(8,128)(2,1)}), bf16[64,64,256]{2,1,0:T(8,128)(2,1)}) %all-gather.13.cloned.1.call-update) | async-done | bytes 2097168 | tf_op jit(solution)/shard_map/all_gather | solution.py:245
  241.9 5.7 %expand_parts.1 = (bf16[192,1024]{1,0:T(8,128)(2,1)S(1)}, bf16[192,1024]{1,0:T(8,128)(2,1)S(1)}, bf16[192,1024]{1,0:T(8,128)(2,1)S(1)}, bf16[192,1024]{1,0:T(8,1...) custom-call(s32[1]{0:T(128)} %bitcast.1.p_ref, ...), custom_call_target="tpu_custom_call" | custom-call | flops 3221225472 | bytes 5242880 | tf_op jit(solution)/shard_map/expand_parts/pallas_call | solution.py:221
  253.5 20.4 %collective-permute-done.16.refs_2_ = bf16[192,1024]{1,0:T(8,128)(2,1)S(1)} collective-permute-done((bf16[192,1024]{1,0:T(8,128)(2,1)S(1)}, bf16[192,1024]{1,0:T(8,128)(2,1)S(1)}, u32[]{:S(2)}, u32[]{:S(2)}) %collective-permute-start.16) | collective-permute-done | bytes 393248 | tf_op jit(solution)/shard_map/ppermute | solution.py:239
  274.4 4.6 %unpack_joint.1 = (bf16[192,8192]{1,0:T(8,128)(2,1)}, bf16[192,1024]{1,0:T(8,128)(2,1)}, bf16[192,1024]{1,0:T(8,128)(2,1)}) custom-call(bf16[8,192,1280]{2,1,0:T(8,128)(2,1)} %all-to-all-done.4.parts_ref), custom_call_target="tpu_custom_call" | custom-call | bytes 7864320 | tf_op jit(solution)/shard_map/unpack_joint/pallas_call | solution.py:388
  281.4 10.3 %collective-permute-done.20.refs_6_ = bf16[192,1024]{1,0:T(8,128)(2,1)S(1)} collective-permute-done((bf16[192,1024]{1,0:T(8,128)(2,1)}, bf16[192,1024]{1,0:T(8,128)(2,1)S(1)}, u32[]{:S(2)}, u32[]{:S(2)}) %collective-permute-start.20) | collective-permute-done | bytes 393248 | tf_op jit(solution)/shard_map/ppermute | solution.py:239
  291.7 7.5 %collective-permute-done.21.refs_7_ = bf16[192,1024]{1,0:T(8,128)(2,1)S(1)} collective-permute-done((bf16[192,1024]{1,0:T(8,128)(2,1)S(1)}, bf16[192,1024]{1,0:T(8,128)(2,1)S(1)}, u32[]{:S(2)}, u32[]{:S(2)}) %collective-permute-start.21) | collective-permute-done | bytes 393248 | tf_op jit(solution)/shard_map/ppermute | solution.py:239
  (101 shorter events, 50.0 us)
Async XLA Ops:
  11.5 13.9 %all-to-all-start.1 = ((s32[16,1,192]{2,1,0:T(1,128)}), s32[16,1,192]{2,1,0:T(1,128)S(1)}, u32[]{:S(2)}, u32[]{:S(2)}) async-start(s32[16,1,192]{2,1,0:T(1,128)} %broadcast_in_dim.11), calls=%async_computation.1 | async-start | bytes 32768 | tf_op jit(solution)/shard_map/all_to_all | solution.py:233
  25.4 99.0 %all-to-all-start = ((bf16[16,192,512]{2,1,0:T(8,128)(2,1)}), bf16[16,192,512]{2,1,0:T(8,128)(2,1)}, u32[]{:S(2)}, u32[]{:S(2)}) async-start(bf16[16,192,512]{2,1,0:T(8,128)(2,1)} %pack.1), calls=%async_computation | async-start | bytes 6291456 | tf_op jit(solution)/shard_map/all_to_all | solution.py:233
  29.9 110.1 %all-gather.9.cloned.1.call-start = ((), (), s32[]{:S(2)}) async-start(), calls=%async_computation.5 | async-start | bytes 2621440 | tf_op jit(solution)/shard_map/all_gather | solution.py:245
  32.0 175.5 %all-gather.11.cloned.1.call-start = ((), (), s32[]{:S(2)}) async-start(), calls=%async_computation.6 | async-start | bytes 3276800 | tf_op jit(solution)/shard_map/all_gather | solution.py:245
  39.7 14.3 %collective-permute-start = (bf16[192,1024]{1,0:T(8,128)(2,1)}, bf16[192,1024]{1,0:T(8,128)(2,1)S(1)}, u32[]{:S(2)}, u32[]{:S(2)}) collective-permute-start(bf16[192,1024]{1,0:T(8,128)(2,1)} %get-tuple-element.55), channel_id=1, source_target_pairs={{0,1},{1,0},{2,3},{3,2},{16,17},{17,16},{18,19},{19,18},{4,5},{5,4... | collective-permute-start | bytes 1179656 | tf_op jit(solution)/shard_map/ppermute | solution.py:239
  39.9 19.6 %collective-permute-start.1 = (bf16[192,1024]{1,0:T(8,128)(2,1)}, bf16[192,1024]{1,0:T(8,128)(2,1)S(1)}, u32[]{:S(2)}, u32[]{:S(2)}) collective-permute-start(bf16[192,1024]{1,0:T(8,128)(2,1)} %get-tuple-element.56), channel_id=1, source_target_pairs={{0,2},{1,3},{2,0},{3,1},{16,18},{17,19},{18,16},{19,17},{4,6},{5,7... | collective-permute-start | bytes 1179656 | tf_op jit(solution)/shard_map/ppermute | solution.py:239
  41.6 49.7 %collective-permute-start.2 = (bf16[192,1024]{1,0:T(8,128)(2,1)}, bf16[192,1024]{1,0:T(8,128)(2,1)S(1)}, u32[]{:S(2)}, u32[]{:S(2)}) collective-permute-start(bf16[192,1024]{1,0:T(8,128)(2,1)} %get-tuple-element.57), channel_id=1, source_target_pairs={{0,3},{1,2},{2,1},{3,0},{16,19},{17,18},{18,17},{19,16},{4,7},{5,6... | collective-permute-start | bytes 1179656 | tf_op jit(solution)/shard_map/ppermute | solution.py:239
  41.6 49.7 %collective-permute-start.3 = (bf16[192,1024]{1,0:T(8,128)(2,1)S(1)}, bf16[192,1024]{1,0:T(8,128)(2,1)S(1)}, u32[]{:S(2)}, u32[]{:S(2)}) collective-permute-start(bf16[192,1024]{1,0:T(8,128)(2,1)S(1)} %get-tuple-element.58), channel_id=1, source_target_pairs={{0,16},{1,17},{2,18},{3,19},{16,0},{17,1},{18,2},{19,3},{4,20},{5,... | collective-permute-start | bytes 1179656 | tf_op jit(solution)/shard_map/ppermute | solution.py:239
  43.1 10.1 %collective-permute-start.7 = (s32[4,192]{1,0:T(4,128)S(1)}, s32[4,192]{1,0:T(4,128)S(1)}, u32[]{:S(2)}, u32[]{:S(2)}) collective-permute-start(s32[4,192]{1,0:T(4,128)S(1)} %bitcast.20), channel_id=1, source_target_pairs={{0,16},{16,0},{1,17},{17,1},{2,18},{18,2},{3,19},{19,3},{4,20},{20... | collective-permute-start | bytes 9224 | tf_op jit(solution)/shard_map/ppermute | solution.py:448
  53.2 38.2 %collective-permute-start.4 = (bf16[192,1024]{1,0:T(8,128)(2,1)S(1)}, bf16[192,1024]{1,0:T(8,128)(2,1)}, u32[]{:S(2)}, u32[]{:S(2)}) collective-permute-start(bf16[192,1024]{1,0:T(8,128)(2,1)S(1)} %get-tuple-element.59), channel_id=1, source_target_pairs={{0,17},{1,16},{2,19},{3,18},{16,1},{17,0},{18,3},{19,2},{4,21},{5,... | collective-permute-start | bytes 1179656 | tf_op jit(solution)/shard_map/ppermute | solution.py:239
  54.0 37.3 %collective-permute-start.5 = (bf16[192,1024]{1,0:T(8,128)(2,1)S(1)}, bf16[192,1024]{1,0:T(8,128)(2,1)}, u32[]{:S(2)}, u32[]{:S(2)}) collective-permute-start(bf16[192,1024]{1,0:T(8,128)(2,1)S(1)} %get-tuple-element.60), channel_id=1, source_target_pairs={{0,18},{1,19},{2,16},{3,17},{16,2},{17,3},{18,0},{19,1},{4,22},{5,... | collective-permute-start | bytes 1179656 | tf_op jit(solution)/shard_map/ppermute | solution.py:239
  59.5 31.8 %collective-permute-start.6 = (bf16[192,1024]{1,0:T(8,128)(2,1)S(1)}, bf16[192,1024]{1,0:T(8,128)(2,1)}, u32[]{:S(2)}, u32[]{:S(2)}) collective-permute-start(bf16[192,1024]{1,0:T(8,128)(2,1)S(1)} %get-tuple-element.61), channel_id=1, source_target_pairs={{0,19},{1,18},{2,17},{3,16},{16,3},{17,2},{18,1},{19,0},{4,23},{5,... | collective-permute-start | bytes 1179656 | tf_op jit(solution)/shard_map/ppermute | solution.py:239
  140.0 31.9 %all-to-all-start.2 = ((bf16[4,4,192,192]{3,2,1,0:T(8,128)(2,1)}), bf16[4,4,192,192]{3,2,1,0:T(8,128)(2,1)}, u32[]{:S(2)}, u32[]{:S(2)}) async-start(bf16[4,4,192,192]{3,2,1,0:T(8,128)(2,1)} %shrink.1), calls=%async_computation.2 | async-start | bytes 3145728 | tf_op jit(solution)/shard_map/all_to_all | solution.py:233
  158.2 12.7 %collective-permute-start.10 = (bf16[192,64]{1,0:T(8,128)(2,1)S(1)}, bf16[192,64]{1,0:T(8,128)(2,1)S(1)}, u32[]{:S(2)}, u32[]{:S(2)}) collective-permute-start(bf16[192,64]{1,0:T(8,128)(2,1)S(1)} %get-tuple-element.79), channel_id=1, source_target_pairs={{0,3},{1,2},{2,1},{3,0},{16,19},{17,18},{18,17},{19,16},{4,7},{5,6... | collective-permute-start | bytes 73736 | tf_op jit(solution)/shard_map/ppermute | solution.py:239
  159.9 11.9 %collective-permute-start.9 = (bf16[192,64]{1,0:T(8,128)(2,1)S(1)}, bf16[192,64]{1,0:T(8,128)(2,1)S(1)}, u32[]{:S(2)}, u32[]{:S(2)}) collective-permute-start(bf16[192,64]{1,0:T(8,128)(2,1)S(1)} %get-tuple-element.78), channel_id=1, source_target_pairs={{0,2},{1,3},{2,0},{3,1},{16,18},{17,19},{18,16},{19,17},{4,6},{5,7... | collective-permute-start | bytes 73736 | tf_op jit(solution)/shard_map/ppermute | solution.py:239
  174.4 22.1 %all-to-all-start.3 = ((bf16[4,192,192]{2,1,0:T(8,128)(2,1)}), bf16[4,192,192]{2,1,0:T(8,128)(2,1)S(1)}, u32[]{:S(2)}, u32[]{:S(2)}) async-start(bf16[4,192,192]{2,1,0:T(8,128)(2,1)} %reduce_sum.24), calls=%async_computation.3 | async-start | bytes 786432 | tf_op jit(solution)/shard_map/all_to_all | solution.py:233
  185.1 56.9 %all-gather.13.cloned.1.call-start = ((), (), s32[]{:S(2)}) async-start(), calls=%async_computation.7 | async-start | bytes 2621440 | tf_op jit(solution)/shard_map/all_gather | solution.py:245
  215.3 59.1 %all-to-all-start.4 = ((bf16[8,192,1280]{2,1,0:T(8,128)(2,1)}), bf16[8,192,1280]{2,1,0:T(8,128)(2,1)}, u32[]{:S(2)}, u32[]{:S(2)}) async-start(bf16[8,192,1280]{2,1,0:T(8,128)(2,1)} %bitcast.18), calls=%async_computation.4 | async-start | bytes 7864320 | tf_op jit(solution)/shard_map/all_to_all | solution.py:233
  247.7 26.3 %collective-permute-start.16 = (bf16[192,1024]{1,0:T(8,128)(2,1)S(1)}, bf16[192,1024]{1,0:T(8,128)(2,1)S(1)}, u32[]{:S(2)}, u32[]{:S(2)}) collective-permute-start(bf16[192,1024]{1,0:T(8,128)(2,1)S(1)} %get-tuple-element.96), channel_id=1, source_target_pairs={{0,2},{1,3},{2,0},{3,1},{16,18},{17,19},{18,16},{19,17},{4,6},{5,7... | collective-permute-start | bytes 1179656 | tf_op jit(solution)/shard_map/ppermute | solution.py:239
  249.1 32.3 %collective-permute-start.17 = (bf16[192,1024]{1,0:T(8,128)(2,1)}, bf16[192,1024]{1,0:T(8,128)(2,1)S(1)}, u32[]{:S(2)}, u32[]{:S(2)}) collective-permute-start(bf16[192,1024]{1,0:T(8,128)(2,1)} %get-tuple-element.97), channel_id=1, source_target_pairs={{0,3},{1,2},{2,1},{3,0},{16,19},{17,18},{18,17},{19,16},{4,7},{5,6... | collective-permute-start | bytes 1179656 | tf_op jit(solution)/shard_map/ppermute | solution.py:239
  249.5 31.9 %collective-permute-start.18 = (bf16[192,1024]{1,0:T(8,128)(2,1)}, bf16[192,1024]{1,0:T(8,128)(2,1)S(1)}, u32[]{:S(2)}, u32[]{:S(2)}) collective-permute-start(bf16[192,1024]{1,0:T(8,128)(2,1)} %get-tuple-element.98), channel_id=1, source_target_pairs={{0,16},{1,17},{2,18},{3,19},{16,0},{17,1},{18,2},{19,3},{4,20},{5,... | collective-permute-start | bytes 1179656 | tf_op jit(solution)/shard_map/ppermute | solution.py:239
  251.0 30.4 %collective-permute-start.19 = (bf16[192,1024]{1,0:T(8,128)(2,1)}, bf16[192,1024]{1,0:T(8,128)(2,1)S(1)}, u32[]{:S(2)}, u32[]{:S(2)}) collective-permute-start(bf16[192,1024]{1,0:T(8,128)(2,1)} %get-tuple-element.99), channel_id=1, source_target_pairs={{0,17},{1,16},{2,19},{3,18},{16,1},{17,0},{18,3},{19,2},{4,21},{5,... | collective-permute-start | bytes 1179656 | tf_op jit(solution)/shard_map/ppermute | solution.py:239
  251.2 40.6 %collective-permute-start.20 = (bf16[192,1024]{1,0:T(8,128)(2,1)}, bf16[192,1024]{1,0:T(8,128)(2,1)S(1)}, u32[]{:S(2)}, u32[]{:S(2)}) collective-permute-start(bf16[192,1024]{1,0:T(8,128)(2,1)} %get-tuple-element.100), channel_id=1, source_target_pairs={{0,18},{1,19},{2,16},{3,17},{16,2},{17,3},{18,0},{19,1},{4,22},{5,... | collective-permute-start | bytes 1179656 | tf_op jit(solution)/shard_map/ppermute | solution.py:239
  273.9 25.3 %collective-permute-start.21 = (bf16[192,1024]{1,0:T(8,128)(2,1)S(1)}, bf16[192,1024]{1,0:T(8,128)(2,1)S(1)}, u32[]{:S(2)}, u32[]{:S(2)}) collective-permute-start(bf16[192,1024]{1,0:T(8,128)(2,1)S(1)} %get-tuple-element.101), channel_id=1, source_target_pairs={{0,19},{1,18},{2,17},{3,16},{16,3},{17,2},{18,1},{19,0},{4,23},{5,... | collective-permute-start | bytes 1179656 | tf_op jit(solution)/shard_map/ppermute | solution.py:239
  (14 other events, 124.3 us)
Sparse Core Ops, SparseCore 0:
  32.3 87.1 all-gather.8
  121.1 60.3 all-gather.10
  196.7 45.1 all-gather.12

commit v3 on v2

--- a/solution.py
+++ b/solution.py
@@ -9,6 +9,7 @@
 
 LANES = 128
 CHUNK = 48
+NOTE_ROWS = 16
 SET = 8
 RANK = 64
 SCALE = 2.0
@@ -53,9 +54,11 @@
 
 
 def shrink_kernel(ranks, ids_ref, tokens_ref, panel_ref, out_ref):
+    sources, rows = out_ref.shape[0], out_ref.shape[2]
+    tokens = tokens_ref[:, :rows, :].reshape(sources * rows, tokens_ref.shape[2])
     low = shrink_rows(
         ids_ref[...],
-        [tokens_ref[...]],
+        [tokens],
         lambda first: [panel_ref[first : first + 4, :ranks]],
         panel_ref.shape[0],
         ranks,
@@ -64,19 +67,20 @@
 
 
 def shrink(ids, tokens, panels, ranks, inner, tok_rows):
-    rows, columns = tokens.shape
+    sources, held_rows, columns = tokens.shape
     adapters, held, _ = panels.shape
     tile = inner * tok_rows
+    steps = sources // inner
     return call(
         functools.partial(shrink_kernel, ranks),
         "shrink",
-        bf16(inner, rows // tile, tok_rows, ranks),
-        2 * rows * columns * ranks * adapters,
-        2 * (rows + adapters * held) * columns,
-        grid=(rows // tile,),
+        bf16(inner, steps, tok_rows, ranks),
+        2 * steps * tile * columns * ranks * adapters,
+        2 * (steps * tile + adapters * held) * columns,
+        grid=(steps,),
         in_specs=[
             pl.BlockSpec((tile, 1), lambda i: (i, 0)),
-            pl.BlockSpec((tile, columns), lambda i: (i, 0)),
+            pl.BlockSpec((inner, held_rows, columns), lambda i: (i, 0, 0)),
             pl.BlockSpec((adapters, held, columns), lambda i: (0, 0, 0)),
         ],
         out_specs=pl.BlockSpec((inner, 1, tok_rows, ranks), lambda i: (0, i, 0, 0)),
@@ -84,7 +88,8 @@
 
 
 def shrink_parts_kernel(ids_ref, panel_ref, *refs):
-    pieces, adapters, ranks, width = panel_ref.shape
+    pieces, adapters, _, width = panel_ref.shape
+    ranks = refs[-1].shape[1]
     members = len(refs) // 2
     rows = refs[0].shape[0]
     for s in range(0, members, 2):
@@ -92,7 +97,7 @@
         low = shrink_rows(
             ids_ref[s * rows : (s + 2) * rows],
             [both[:, k * width : (k + 1) * width] for k in range(pieces)],
-            lambda first: [panel_ref[k, first : first + 4] for k in range(pieces)],
+            lambda first: [panel_ref[k, first : first + 4, :ranks] for k in range(pieces)],
             adapters,
             ranks,
         ).astype(jnp.bfloat16)
@@ -100,9 +105,9 @@
         refs[members + s + 1][...] = low[rows:]
 
 
-def shrink_parts(ids, tokens, panels):
+def shrink_parts(ids, tokens, panels, ranks):
     members, (rows, columns) = len(tokens), tokens[0].shape
-    pieces, adapters, ranks, width = panels.shape
+    adapters = panels.shape[1]
     vmem = pl.BlockSpec(memory_space=pltpu.VMEM)
     return call(
         shrink_parts_kernel,
@@ -151,23 +156,25 @@
     )(ids, low, panels)
 
 
-def expand_joint_kernel(g_ref, ids_ref, low_ref, panel_ref, out_ref):
-    pieces, adapters, folded, width = panel_ref.shape
-    ranks = low_ref.shape[1] // 3
-    rows = folded - ranks
+def expand_joint_kernel(start, g_ref, ids_ref, low_ref, panel_ref, out_ref):
+    pieces, adapters, held, width = panel_ref.shape
+    ranks = low_ref.shape[1] // 4
+    stop = start + ranks
+    rows = held - stop
     narrow = rows * width // ranks
     ids = ids_ref[...]
     spread = spread_rows(ids, low_ref[:, :ranks], adapters)
     for k in range(pieces):
-        panel = panel_ref[k, :, :ranks].reshape(adapters * ranks, width)
+        panel = panel_ref[k, :, start:stop].reshape(adapters * ranks, width)
         full = jnp.dot(spread, panel, preferred_element_type=jnp.float32)
         out_ref[:, k * width : (k + 1) * width] = (SCALE * full).astype(out_ref.dtype)
-    low_kv = jnp.where(g_ref[0] == 0, low_ref[:, ranks : 2 * ranks], low_ref[:, 2 * ranks :])
+    low_kv = [low_ref[:, j * ranks : (j + 1) * ranks] for j in (1, 2)]
+    low_kv = jnp.where(g_ref[0] == 0, *low_kv)
     spread = spread_rows(ids, low_kv, adapters)
     wide = []
     for k in range(pieces):
         parts = [
-            panel_ref[k, :, ranks:, j * narrow : (j + 1) * narrow]
+            panel_ref[k, :, stop:, j * narrow : (j + 1) * narrow]
             for j in range(ranks // rows)
         ]
         wide.append(jnp.concatenate(parts, axis=1))
@@ -176,12 +183,12 @@
     out_ref[:, pieces * width :] = (SCALE * full).astype(out_ref.dtype)
 
 
-def expand_joint(g, ids, low, panels, tile):
-    rows, ranks = low.shape[0], low.shape[1] // 3
-    pieces, adapters, folded, width = panels.shape
-    columns = pieces * (width + (folded - ranks) * width // ranks)
-    return call(
-        expand_joint_kernel,
+def expand_joint(g, ids, low, panels, start, tile):
+    rows, ranks = low.shape[0], low.shape[1] // 4
+    pieces, adapters, held, width = panels.shape
+    columns = pieces * (width + (held - start - ranks) * width // ranks)
+    return call(
+        functools.partial(expand_joint_kernel, start),
         "expand_joint",
         bf16(rows, columns),
         2 * rows * columns * ranks * adapters,
@@ -190,7 +197,7 @@
         in_specs=[
             pl.BlockSpec(memory_space=pltpu.SMEM),
             pl.BlockSpec((tile, 1), lambda i: (i, 0)),
-            pl.BlockSpec((tile, 3 * ranks), lambda i: (i, 0)),
+            pl.BlockSpec((tile, 4 * ranks), lambda i: (i, 0)),
             pl.BlockSpec(panels.shape, lambda i: (0, 0, 0, 0)),
         ],
         out_specs=pl.BlockSpec((tile, columns), lambda i: (i, 0)),
@@ -199,9 +206,9 @@
 
 def expand_parts_kernel(p_ref, ids_ref, low_ref, panel_ref, *out_refs):
     pieces, adapters, ranks, width = panel_ref.shape
-    rows = low_ref.shape[1]
+    rows, start = low_ref.shape[1], low_ref.shape[2] - ranks
     for s in range(0, len(out_refs), 2):
-        pair = [low_ref[p_ref[0] ^ s], low_ref[p_ref[0] ^ (s + 1)]]
+        pair = [low_ref[p_ref[0] ^ (s + j), :, start:] for j in range(2)]
         spread = spread_rows(
             ids_ref[s * rows : (s + 2) * rows], jnp.concatenate(pair, axis=0), adapters
         )
@@ -214,8 +221,8 @@
 
 
 def expand_parts(p, ids, low, panels):
-    members, rows, ranks = low.shape
-    pieces, adapters, _, width = panels.shape
+    members, rows, _ = low.shape
+    pieces, adapters, ranks, width = panels.shape
     columns = pieces * width
     vmem = pl.BlockSpec(memory_space=pltpu.VMEM)
     return call(
@@ -345,25 +352,37 @@
     )(array)
 
 
-def pack_kernel(source_ref, out_ref):
-    width = out_ref.shape[2]
-    for m in range(out_ref.shape[0]):
-        out_ref[m] = source_ref[:, m * width : (m + 1) * width]
-
-
-def pack(array, members):
+def pack_kernel(steps, notes_ref, source_ref, out_ref):
+    members, _, width = out_ref.shape
+
+    @pl.when(pl.program_id(0) < steps)
+    def _():
+        for m in range(members):
+            out_ref[m] = source_ref[:, m * width : (m + 1) * width]
+
+    @pl.when(pl.program_id(0) == steps)
+    def _():
+        for m in range(members):
+            out_ref[m] = notes_ref[...]
+
+
+def pack(array, notes, members):
     rows, columns = array.shape
-    width = columns // members
-    return call(
-        pack_kernel,
+    chunk, width = notes.shape
+    steps = rows // chunk
+    return call(
+        functools.partial(pack_kernel, steps),
         "pack",
-        bf16(members, rows, width),
+        bf16(members, rows + chunk, width),
         0,
         4 * array.size,
-        grid=(rows // CHUNK,),
-        in_specs=[pl.BlockSpec((CHUNK, columns), lambda i: (i, 0))],
-        out_specs=pl.BlockSpec((members, CHUNK, width), lambda i: (0, i, 0)),
-    )(array)
+        grid=(steps + 1,),
+        in_specs=[
+            pl.BlockSpec((chunk, width), lambda i: (0, 0)),
+            pl.BlockSpec((chunk, columns), lambda i: (jnp.minimum(i, steps - 1), 0)),
+        ],
+        out_specs=pl.BlockSpec((members, chunk, width), lambda i: (0, i, 0)),
+    )(notes, array)
 
 
 def unpack_joint_kernel(count, inner, groups, narrow, parts_ref, q_ref, k_ref, v_ref):
@@ -426,24 +445,43 @@
         width = panel.shape[2] // groups
         return lax.dynamic_slice_in_dim(panel, g * width, width, 2)
 
+    def finish_o(low_o, b_o):
+        full_o = expand_parts(p, swap_ids, low_o, b_o)
+        return unpack_parts(swap_parts(full_o), p, count, inner, groups)
+
+    owner = send_slot // slot_rows
+    at_owner = owner[:, None] == jnp.arange(devices)[None, :]
+    listed = jnp.any(fetch_list[None] == adapter_ids[:, None, None], axis=2)
+    own_ids = jnp.where(jnp.any(at_owner & listed, axis=1), adapter_ids, -1)
+    notes = jnp.broadcast_to(own_ids.astype(jnp.bfloat16), (NOTE_ROWS, tok_rows))
+    notes = jnp.pad(notes, ((0, 0), (0, normed_hidden.shape[1] // devices - tok_rows)))
+    packed_x = pack(normed_hidden, notes, devices)
+    sent_x = exchange(packed_x, REQ)
+
+    attn_mixed, packed_x = lax.optimization_barrier((attn_mixed, packed_x))
+    sent_y = swap_parts(pack_parts(attn_mixed, p, count, inner, groups))
+    a_o = along_h(own_columns(shrink_panels[:, 3 * RANK :]))
     own_q = own_columns(expand_qo[:, :RANK])
     fold = groups == 2 and own_q.shape[2] % LANES == 0
     if fold:
         own_kv = lax.dynamic_slice_in_dim(expand_kv, g * RANK, RANK, 1)
         folds = own_q.shape[2] // own_kv.shape[2]
         own_kv = jnp.concatenate(jnp.split(own_kv, folds, axis=1), axis=2)
-        b_q = along_h(jnp.concatenate([own_q, own_kv], axis=1))
+        own_q = jnp.concatenate([own_q, own_kv], axis=1)
     else:
-        b_q = along_h(own_q)
         b_kv = along_h(own_columns(expand_kv))
-
-    a_o = along_h(own_columns(shrink_panels[:, 3 * RANK :]))
-
-    listed = fetch_list[send_slot // slot_rows]
-    keep = jnp.any(listed == adapter_ids[:, None], axis=1)
-    own_ids = jnp.where(keep, adapter_ids, -1)
-    group_ids = exchange(jnp.broadcast_to(own_ids, (devices, tok_rows)), REQ)
+    own_q, sent_y = lax.optimization_barrier((own_q, sent_y))
+    b_q = along_h(own_q)
+
+    sent_x, sent_y = lax.optimization_barrier((sent_x, sent_y))
+
+    group_ids = sent_x[:, tok_rows, :tok_rows].astype(jnp.int32)
     near_ids = lax.dynamic_slice_in_dim(group_ids, h * inner, inner, 0)
+    group_ids = group_ids.reshape(devices * tok_rows, 1)
+    part = shrink(group_ids, sent_x, shrink_panels, 3 * RANK, inner, tok_rows)
+    part, near_ids = lax.optimization_barrier((part, near_ids))
+    near = jnp.sum(exchange(part, "r").astype(jnp.float32), axis=0).astype(jnp.bfloat16)
+
     if groups == 2:
         far_ids = lax.ppermute(near_ids, "groups", [(0, 1), (1, 0)])
         first, second = jnp.where(g == 0, near_ids, far_ids), jnp.where(g == 0, far_ids, near_ids)
@@ -452,52 +490,34 @@
         plane_ids = lax.all_gather(near_ids, "groups", axis=0, tiled=True)
     swap_ids = plane_ids[p ^ jnp.arange(members)].reshape(rows, 1)
     plane_ids = plane_ids.reshape(rows, 1)
-    group_ids = group_ids.reshape(devices * tok_rows, 1)
-
-    packed_x = pack(normed_hidden, devices)
-    sent_x = exchange(packed_x, REQ)
-    attn_mixed, packed_x = lax.optimization_barrier((attn_mixed, packed_x))
-    sent_y = swap_parts(pack_parts(attn_mixed, p, count, inner, groups))
-
-    sent_x, sent_y, group_ids, swap_ids, plane_ids = lax.optimization_barrier(
-        (sent_x, sent_y, group_ids, swap_ids, plane_ids)
-    )
-    tokens = sent_x.reshape(devices * tok_rows, -1)
-    part = shrink(group_ids, tokens, shrink_panels, 3 * RANK, inner, tok_rows)
-    part, a_o = lax.optimization_barrier((part, a_o))
-    near = jnp.sum(exchange(part, "r").astype(jnp.float32), axis=0).astype(jnp.bfloat16)
-
-    parts_o = swap_parts(shrink_parts(swap_ids, sent_y, a_o))
+    parts_o = shrink_parts(swap_ids, sent_y, a_o, RANK)
+    near, parts_o = lax.optimization_barrier((near, parts_o))
+    far = exchange(near, "h")
+    parts_o = swap_parts(parts_o)
     low_o = sum(piece.astype(jnp.float32) for piece in parts_o).astype(jnp.bfloat16)
-    near, low_o = lax.optimization_barrier((near, low_o))
-    low_o = lax.all_gather(low_o, PLANE, axis=0)
-
-    far = exchange(near, "h")
-    far, low_o, own_o = lax.optimization_barrier((far, low_o, own_columns(expand_qo[:, RANK:])))
+    low = jnp.sum(far.astype(jnp.float32), axis=0).astype(jnp.bfloat16)
+    low, own_o = lax.optimization_barrier((low, own_columns(expand_qo[:, RANK:])))
     b_o = along_h(own_o)
-    low = jnp.sum(far.astype(jnp.float32), axis=0).astype(jnp.bfloat16)
+    low = jnp.concatenate([low, low_o], axis=1)
     low = lax.all_gather(low, PLANE, axis=0, tiled=True)
+    low_all = low.reshape(members, tok_rows, -1)
 
     def home(low_part, panels):
         full = expand(plane_ids, low_part, panels, tile)
         return exchange(full.reshape(members, tok_rows, -1), PLANE)
 
     if fold:
-        full = expand_joint(g.reshape(1), plane_ids, low, b_q, tile)
-        full, low_o = lax.optimization_barrier((full, low_o))
+        full = expand_joint(g.reshape(1), plane_ids, low, b_q, 0, tile)
+        full, low_all = lax.optimization_barrier((full, low_all))
         parts = exchange(full.reshape(members, tok_rows, -1), PLANE)
         narrow = expand_kv.shape[2]
         delta_q, delta_k, delta_v = unpack_joint(parts, narrow, count, inner, groups)
-        full_o = expand_parts(p, swap_ids, low_o, b_o)
-        delta_o = unpack_parts(swap_parts(full_o), p, count, inner, groups)
-        return delta_q, delta_k, delta_v, delta_o
-    full_o = expand_parts(p, swap_ids, low_o, b_o)
-    delta_o = unpack_parts(swap_parts(full_o), p, count, inner, groups)
-    low_k, low_v = low[:, RANK : 2 * RANK], low[:, 2 * RANK :]
+        return delta_q, delta_k, delta_v, finish_o(low_all, b_o)
+    low_k, low_v = low[:, RANK : 2 * RANK], low[:, 2 * RANK : 3 * RANK]
     delta_k = unpack(home(low_k, b_kv[:, :, :RANK]), count, inner, groups)
     delta_v = unpack(home(low_v, b_kv[:, :, RANK:]), count, inner, groups)
     delta_q = unpack(home(low[:, :RANK], b_q), count, inner, groups)
-    return delta_q, delta_k, delta_v, delta_o
+    return delta_q, delta_k, delta_v, finish_o(low_all, b_o)
 
 
 def solution(mesh):

time: 309 us -> 306 us (level)
  local copies, waits for them, and re-layouts: 14.3 us -> 24.3 us
  blocking collectives: 19.8 us -> 10.4 us
    all_gather x1 -> x0, blocking collectives: 9.28 us -> none  [shards(): low_o = lax.all_gather(low_o, PLANE, axis=0)]
    unnamed x21 -> x29, local copies, waits for them, and re-layouts: 3.69 us -> 12.5 us
    all_to_all x5 -> x4, waiting for transfers between devices: 36.5 us -> 44.4 us  [exchange(): return lax.all_to_all(array, axes, split_axis=0, concat_axis=0, tiled=True)]
    ppermute x1, waiting for transfers between devices: 9.52 us -> 2.1 us  [shards(): far_ids = lax.ppermute(near_ids, 'groups', [(0, 1), (1, 0)])]
    all_to_all x5 -> x4, starting transfers between devices: 33.4 us -> 31.4 us  [exchange(): return lax.all_to_all(array, axes, split_axis=0, concat_axis=0, tiled=True)]
  transfers between devices with their start and end apart: 30 -> 29, of which waited for: 14 -> 12; matrix products, arithmetic and copies ran while one was open for 5% -> 7% of each run, Pallas kernels for 14% -> 13%
where the time goes in v3:
time: 306 us; the launch traced here: 305 us
  waiting for transfers between devices  149 us (49%)
  starting transfers between devices  51.6 us (17%)
  Pallas kernels  47.4 us (15%)
  local copies, waits for them, and re-layouts  24.3 us (8%)
  between operations  14 us (5%)
  blocking collectives  10.4 us (3%)
  other arithmetic  8.57 us (3%)
    ppermute x21, waiting for transfers between devices, swap_parts(): lax.ppermute(parts[s], PLANE, [(d, d ^ s) for d in range(members)])  80.5 us
    all_to_all x4, waiting for transfers between devices, exchange(): return lax.all_to_all(array, axes, split_axis=0, concat_axis=0, tiled=True)  44.4 us
    all_to_all x4, starting transfers between devices, exchange(): return lax.all_to_all(array, axes, split_axis=0, concat_axis=0, tiled=True)  31.4 us
    all_gather x3, waiting for transfers between devices, along_h(): pieces = lax.all_gather(array, 'h', axis=0)  21.5 us
    ppermute x21, starting transfers between devices, swap_parts(): lax.ppermute(parts[s], PLANE, [(d, d ^ s) for d in range(members)])  18.6 us
    pallas_call x1, Pallas kernels, shrink(): call(functools.partial(shrink_kernel, ranks), 'shrink', bf16(inner, steps...  14.5 us
    unnamed x29, local copies, waits for them, and re-layouts  12.5 us
    all_gather x1, blocking collectives, shards(): low = lax.all_gather(low, PLANE, axis=0, tiled=True)  10.4 us
  transfers between devices with their start and end apart: 29, of which 12 were waited for; matrix products, arithmetic and copies ran while one was open for 7% of the time, Pallas kernels for 13%

profile of v3, /device:TPU:0, one launch (start us, length us, event | category | flops | bytes accessed | tf_op | source)
XLA Modules:
  0.0 304.9 jit_solution(955458220761791019)
XLA Ops:
  11.2 5.2 %pack.1 = bf16[16,208,512]{2,1,0:T(8,128)(2,1)} custom-call(bf16[16,512]{1,0:T(8,128)(2,1)S(1)} %pad.7.notes_ref, bf16[192,8192]{1,0:T(8,128)(2,1)S(1)} %copy-done), custom_call_target="tpu_custom_call" | custom-call | bytes 6291456 | tf_op jit(solution)/shard_map/pack/pallas_call | solution.py:373
  16.5 7.4 %all-to-all-start = ((bf16[16,208,512]{2,1,0:T(8,128)(2,1)}), bf16[16,208,512]{2,1,0:T(8,128)(2,1)}, u32[]{:S(2)}, u32[]{:S(2)}) async-start(bf16[16,208,512]{2,1,0:T(8,128)(2,1)} %pack.1), calls=%async_computation | async-start | bytes 6815744 | tf_op jit(solution)/shard_map/all_to_all | solution.py:240
  26.1 4.0 %pack_parts.1 = (bf16[192,1024]{1,0:T(8,128)(2,1)S(1)}, bf16[192,1024]{1,0:T(8,128)(2,1)S(1)}, bf16[192,1024]{1,0:T(8,128)(2,1)S(1)}, bf16[192,1024]{1,0:T(8,128...) custom-call(s32[1]{0:T(128)} %bitcast.1.p_ref, ...), custom_call_target="tpu_custom_call" | custom-call | bytes 6291456 | tf_op jit(solution)/shard_map/pack_parts/pallas_call | solution.py:284
  34.0 3.3 %fusion.4 = (bf16[16,64,512]{2,1,0:T(8,128)(2,1)}, bf16[16,64,512]{2,1,0:T(8,128)(2,1)}) fusion(bf16[16,128,512]{2,1,0:T(8,128)(2,1)} %param.15), kind=kLoop, calls=%fused_computation.27 | loop fusion | bytes 4194304 | tf_op jit(solution)/shard_map/slice | solution.py:499
  37.3 2.6 collective-permute-start.5
  39.9 24.7 %collective-permute-done.1.refs_2_ = bf16[192,1024]{1,0:T(8,128)(2,1)S(1)} collective-permute-done((bf16[192,1024]{1,0:T(8,128)(2,1)S(1)}, bf16[192,1024]{1,0:T(8,128)(2,1)S(1)}, u32[]{:S(2)}, u32[]{:S(2)}) %collective-permute-start.1) | collective-permute-done | bytes 393248 | tf_op jit(solution)/shard_map/ppermute | solution.py:246
  73.4 14.2 %collective-permute-done.2.refs_3_ = bf16[192,1024]{1,0:T(8,128)(2,1)S(1)} collective-permute-done((bf16[192,1024]{1,0:T(8,128)(2,1)}, bf16[192,1024]{1,0:T(8,128)(2,1)S(1)}, u32[]{:S(2)}, u32[]{:S(2)}) %collective-permute-start.2) | collective-permute-done | bytes 393248 | tf_op jit(solution)/shard_map/ppermute | solution.py:246
  89.9 31.6 %all-to-all-done.tokens_ref = bf16[16,208,512]{2,1,0:T(8,128)(2,1)} async-done(((bf16[16,208,512]{2,1,0:T(8,128)(2,1)}), bf16[16,208,512]{2,1,0:T(8,128)(2,1)}, u32[]{:S(2)}, u32[]{:S(2)}) %all-to-all-start) | async-done | bytes 3407904 | tf_op jit(solution)/shard_map/all_to_all | solution.py:240
  124.8 14.5 %shrink.1 = bf16[4,4,192,192]{3,2,1,0:T(8,128)(2,1)} custom-call(s32[3072,1]{1,0:T(8,128)S(1)} %reshape.79.ids_ref, bf16[16,208,512]{2,1,0:T(8,128)(2,1)} %all-to-all-done.tokens_ref, bf16[16,256,512]{2,1,0:T(8,128)(2,1)} %panel_ref.1), custom_call_target="tpu_custom_call" | custom-call | flops 9663676416 | bytes 7340032 | tf_op jit(solution)/shard_map/shrink/pallas_call | solution.py:74
  139.3 7.0 %all-to-all-start.1 = ((bf16[4,4,192,192]{3,2,1,0:T(8,128)(2,1)}), bf16[4,4,192,192]{3,2,1,0:T(8,128)(2,1)}, u32[]{:S(2)}, u32[]{:S(2)}) async-start(bf16[4,4,192,192]{3,2,1,0:T(8,128)(2,1)} %shrink.1), calls=%async_computation.1 | async-start | bytes 3145728 | tf_op jit(solution)/shard_map/all_to_all | solution.py:240
  153.1 5.2 %shrink_parts.1 = (bf16[192,64]{1,0:T(8,128)(2,1)S(1)}, bf16[192,64]{1,0:T(8,128)(2,1)S(1)}, bf16[192,64]{1,0:T(8,128)(2,1)S(1)}, bf16[192,64]{1,0:T(8,128)(2,1)...) custom-call(s32[1536,1]{1,0:T(8,128)S(1)} %reshape.81.ids_ref, ...), custom_call_target="tpu_custom_call" | custom-call | flops 3221225472 | bytes 5242880 | tf_op jit(solution)/shard_map/shrink_parts/pallas_call | solution.py:112
  158.3 9.0 %all-to-all-done.1 = bf16[4,4,192,192]{3,2,1,0:T(8,128)(2,1)} async-done(((bf16[4,4,192,192]{3,2,1,0:T(8,128)(2,1)}), bf16[4,4,192,192]{3,2,1,0:T(8,128)(2,1)}, u32[]{:S(2)}, u32[]{:S(2)}) %all-to-all-start.1) | async-done | bytes 1179680 | tf_op jit(solution)/shard_map/all_to_all | solution.py:240
  167.3 2.5 reduce_sum.24
  169.9 12.4 %all-to-all-start.2 = ((bf16[4,192,192]{2,1,0:T(8,128)(2,1)}), bf16[4,192,192]{2,1,0:T(8,128)(2,1)S(1)}, u32[]{:S(2)}, u32[]{:S(2)}) async-start(bf16[4,192,192]{2,1,0:T(8,128)(2,1)} %reduce_sum.24), calls=%async_computation.2 | async-start | bytes 786432 | tf_op jit(solution)/shard_map/all_to_all | solution.py:240
  190.0 3.8 %all-to-all-done.2 = bf16[4,192,192]{2,1,0:T(8,128)(2,1)S(1)} async-done(((bf16[4,192,192]{2,1,0:T(8,128)(2,1)}), bf16[4,192,192]{2,1,0:T(8,128)(2,1)S(1)}, u32[]{:S(2)}, u32[]{:S(2)}) %all-to-all-start.2) | async-done | bytes 294944 | tf_op jit(solution)/shard_map/all_to_all | solution.py:240
  194.1 10.4 %all_gather.23.low_ref = bf16[1536,256]{1,0:T(8,128)(2,1)S(1)} all-gather(bf16[192,256]{1,0:T(8,128)(2,1)S(1)} %pad_maximum_fusion), channel_id=1, replica_groups=mesh['groups'=2,'h'=4,'r'=4] {'groups','r'}, dimensions={0}, use_global_device_ids=true | all-gather | bytes 884736 | tf_op jit(solution)/shard_map/all_gather | solution.py:502
  206.3 5.9 %expand_joint.1 = bf16[1536,1280]{1,0:T(8,128)(2,1)} custom-call(s32[1]{0:T(128)} %bitcast.g_ref, s32[1536,1]{1,0:T(8,128)S(1)} %reshape.80.ids_ref, bf16[1536,256]{1,0:T(8,128)(2,1)S(1)} %all_gather.23.low_ref, bf16[4,16,80,256]{3,2,1,0:T(8,128)(2,1)S(1)} %bitcast.13), custom_call_target="tpu_custom_call" | custom-call | flops 4026531840 | bytes 6553600 | tf_op jit(solution)/shard_map/expand_joint/pallas_call | solution.py:190
  212.2 4.5 %all-to-all-start.3 = ((bf16[8,192,1280]{2,1,0:T(8,128)(2,1)}), bf16[8,192,1280]{2,1,0:T(8,128)(2,1)}, u32[]{:S(2)}, u32[]{:S(2)}) async-start(bf16[8,192,1280]{2,1,0:T(8,128)(2,1)} %bitcast.14), calls=%async_computation.3 | async-start | bytes 7864320 | tf_op jit(solution)/shard_map/all_to_all | solution.py:240
  216.7 21.5 %all-gather.11.cloned.1.call-done = bf16[64,64,256]{2,1,0:T(8,128)(2,1)} async-done(((bf16[16,64,256]{2,1,0:T(8,128)(2,1)}), bf16[64,64,256]{2,1,0:T(8,128)(2,1)}) %all-gather.11.cloned.1.call-update) | async-done | bytes 2097168 | tf_op jit(solution)/shard_map/all_gather | solution.py:252
  238.2 5.8 %expand_parts.1 = (bf16[192,1024]{1,0:T(8,128)(2,1)S(1)}, bf16[192,1024]{1,0:T(8,128)(2,1)S(1)}, bf16[192,1024]{1,0:T(8,128)(2,1)S(1)}, bf16[192,1024]{1,0:T(8,1...) custom-call(s32[1]{0:T(128)} %bitcast.1.p_ref, ...), custom_call_target="tpu_custom_call" | custom-call | flops 3221225472 | bytes 5242880 | tf_op jit(solution)/shard_map/expand_parts/pallas_call | solution.py:228
  249.8 21.0 %collective-permute-done.16.refs_2_ = bf16[192,1024]{1,0:T(8,128)(2,1)S(1)} collective-permute-done((bf16[192,1024]{1,0:T(8,128)(2,1)S(1)}, bf16[192,1024]{1,0:T(8,128)(2,1)S(1)}, u32[]{:S(2)}, u32[]{:S(2)}) %collective-permute-start.16) | collective-permute-done | bytes 393248 | tf_op jit(solution)/shard_map/ppermute | solution.py:246
  271.3 4.6 %unpack_joint.1 = (bf16[192,8192]{1,0:T(8,128)(2,1)}, bf16[192,1024]{1,0:T(8,128)(2,1)}, bf16[192,1024]{1,0:T(8,128)(2,1)}) custom-call(bf16[8,192,1280]{2,1,0:T(8,128)(2,1)} %all-to-all-done.3.parts_ref), custom_call_target="tpu_custom_call" | custom-call | bytes 7864320 | tf_op jit(solution)/shard_map/unpack_joint/pallas_call | solution.py:407
  278.3 10.3 %collective-permute-done.20.refs_6_ = bf16[192,1024]{1,0:T(8,128)(2,1)S(1)} collective-permute-done((bf16[192,1024]{1,0:T(8,128)(2,1)}, bf16[192,1024]{1,0:T(8,128)(2,1)S(1)}, u32[]{:S(2)}, u32[]{:S(2)}) %collective-permute-start.20) | collective-permute-done | bytes 393248 | tf_op jit(solution)/shard_map/ppermute | solution.py:246
  288.6 7.5 %collective-permute-done.21.refs_7_ = bf16[192,1024]{1,0:T(8,128)(2,1)S(1)} collective-permute-done((bf16[192,1024]{1,0:T(8,128)(2,1)S(1)}, bf16[192,1024]{1,0:T(8,128)(2,1)S(1)}, u32[]{:S(2)}, u32[]{:S(2)}) %collective-permute-start.21) | collective-permute-done | bytes 393248 | tf_op jit(solution)/shard_map/ppermute | solution.py:246
  (104 shorter events, 51.9 us)
Async XLA Ops:
  16.5 105.1 %all-to-all-start = ((bf16[16,208,512]{2,1,0:T(8,128)(2,1)}), bf16[16,208,512]{2,1,0:T(8,128)(2,1)}, u32[]{:S(2)}, u32[]{:S(2)}) async-start(bf16[16,208,512]{2,1,0:T(8,128)(2,1)} %pack.1), calls=%async_computation | async-start | bytes 6815744 | tf_op jit(solution)/shard_map/all_to_all | solution.py:240
  23.9 127.2 %all-gather.7.cloned.1.call-start = ((), (), s32[]{:S(2)}) async-start(), calls=%async_computation.4 | async-start | bytes 2621440 | tf_op jit(solution)/shard_map/all_gather | solution.py:252
  26.1 178.5 %all-gather.9.cloned.1.call-start = ((), (), s32[]{:S(2)}) async-start(), calls=%async_computation.5 | async-start | bytes 3276800 | tf_op jit(solution)/shard_map/all_gather | solution.py:252
  30.1 7.1 %collective-permute-start = (bf16[192,1024]{1,0:T(8,128)(2,1)S(1)}, bf16[192,1024]{1,0:T(8,128)(2,1)S(1)}, u32[]{:S(2)}, u32[]{:S(2)}) collective-permute-start(bf16[192,1024]{1,0:T(8,128)(2,1)S(1)} %get-tuple-element.67), channel_id=1, source_target_pairs={{0,1},{1,0},{2,3},{3,2},{16,17},{17,16},{18,19},{19,18},{4,5},{5,4... | collective-permute-start | bytes 1179656 | tf_op jit(solution)/shard_map/ppermute | solution.py:246
  30.5 34.1 %collective-permute-start.1 = (bf16[192,1024]{1,0:T(8,128)(2,1)S(1)}, bf16[192,1024]{1,0:T(8,128)(2,1)S(1)}, u32[]{:S(2)}, u32[]{:S(2)}) collective-permute-start(bf16[192,1024]{1,0:T(8,128)(2,1)S(1)} %get-tuple-element.68), channel_id=1, source_target_pairs={{0,2},{1,3},{2,0},{3,1},{16,18},{17,19},{18,16},{19,17},{4,6},{5,7... | collective-permute-start | bytes 1179656 | tf_op jit(solution)/shard_map/ppermute | solution.py:246
  32.2 55.4 %collective-permute-start.2 = (bf16[192,1024]{1,0:T(8,128)(2,1)}, bf16[192,1024]{1,0:T(8,128)(2,1)S(1)}, u32[]{:S(2)}, u32[]{:S(2)}) collective-permute-start(bf16[192,1024]{1,0:T(8,128)(2,1)} %get-tuple-element.69), channel_id=1, source_target_pairs={{0,3},{1,2},{2,1},{3,0},{16,19},{17,18},{18,17},{19,16},{4,7},{5,6... | collective-permute-start | bytes 1179656 | tf_op jit(solution)/shard_map/ppermute | solution.py:246
  32.2 55.4 %collective-permute-start.3 = (bf16[192,1024]{1,0:T(8,128)(2,1)}, bf16[192,1024]{1,0:T(8,128)(2,1)S(1)}, u32[]{:S(2)}, u32[]{:S(2)}) collective-permute-start(bf16[192,1024]{1,0:T(8,128)(2,1)} %get-tuple-element.70), channel_id=1, source_target_pairs={{0,16},{1,17},{2,18},{3,19},{16,0},{17,1},{18,2},{19,3},{4,20},{5,... | collective-permute-start | bytes 1179656 | tf_op jit(solution)/shard_map/ppermute | solution.py:246
  33.7 54.0 %collective-permute-start.4 = (bf16[192,1024]{1,0:T(8,128)(2,1)}, bf16[192,1024]{1,0:T(8,128)(2,1)S(1)}, u32[]{:S(2)}, u32[]{:S(2)}) collective-permute-start(bf16[192,1024]{1,0:T(8,128)(2,1)} %get-tuple-element.71), channel_id=1, source_target_pairs={{0,17},{1,16},{2,19},{3,18},{16,1},{17,0},{18,3},{19,2},{4,21},{5,... | collective-permute-start | bytes 1179656 | tf_op jit(solution)/shard_map/ppermute | solution.py:246
  37.3 51.1 %collective-permute-start.5 = (bf16[192,1024]{1,0:T(8,128)(2,1)}, bf16[192,1024]{1,0:T(8,128)(2,1)S(1)}, u32[]{:S(2)}, u32[]{:S(2)}) collective-permute-start(bf16[192,1024]{1,0:T(8,128)(2,1)} %get-tuple-element.72), channel_id=1, source_target_pairs={{0,18},{1,19},{2,16},{3,17},{16,2},{17,3},{18,0},{19,1},{4,22},{5,... | collective-permute-start | bytes 1179656 | tf_op jit(solution)/shard_map/ppermute | solution.py:246
  64.6 24.6 %collective-permute-start.6 = (bf16[192,1024]{1,0:T(8,128)(2,1)}, bf16[192,1024]{1,0:T(8,128)(2,1)S(1)}, u32[]{:S(2)}, u32[]{:S(2)}) collective-permute-start(bf16[192,1024]{1,0:T(8,128)(2,1)} %get-tuple-element.73), channel_id=1, source_target_pairs={{0,19},{1,18},{2,17},{3,16},{16,3},{17,2},{18,1},{19,0},{4,23},{5,... | collective-permute-start | bytes 1179656 | tf_op jit(solution)/shard_map/ppermute | solution.py:246
  139.3 28.1 %all-to-all-start.1 = ((bf16[4,4,192,192]{3,2,1,0:T(8,128)(2,1)}), bf16[4,4,192,192]{3,2,1,0:T(8,128)(2,1)}, u32[]{:S(2)}, u32[]{:S(2)}) async-start(bf16[4,4,192,192]{3,2,1,0:T(8,128)(2,1)} %shrink.1), calls=%async_computation.1 | async-start | bytes 3145728 | tf_op jit(solution)/shard_map/all_to_all | solution.py:240
  169.9 23.9 %all-to-all-start.2 = ((bf16[4,192,192]{2,1,0:T(8,128)(2,1)}), bf16[4,192,192]{2,1,0:T(8,128)(2,1)S(1)}, u32[]{:S(2)}, u32[]{:S(2)}) async-start(bf16[4,192,192]{2,1,0:T(8,128)(2,1)} %reduce_sum.24), calls=%async_computation.2 | async-start | bytes 786432 | tf_op jit(solution)/shard_map/all_to_all | solution.py:240
  182.3 55.9 %all-gather.11.cloned.1.call-start = ((), (), s32[]{:S(2)}) async-start(), calls=%async_computation.6 | async-start | bytes 2621440 | tf_op jit(solution)/shard_map/all_gather | solution.py:252
  184.2 9.7 %collective-permute-start.12 = (bf16[192,64]{1,0:T(8,128)(2,1)S(1)}, bf16[192,64]{1,0:T(8,128)(2,1)S(1)}, u32[]{:S(2)}, u32[]{:S(2)}) collective-permute-start(bf16[192,64]{1,0:T(8,128)(2,1)S(1)} %get-tuple-element.108), channel_id=1, source_target_pairs={{0,17},{1,16},{2,19},{3,18},{16,1},{17,0},{18,3},{19,2},{4,21},{5,... | collective-permute-start | bytes 73736 | tf_op jit(solution)/shard_map/ppermute | solution.py:246
  186.2 7.7 %collective-permute-start.11 = (bf16[192,64]{1,0:T(8,128)(2,1)S(1)}, bf16[192,64]{1,0:T(8,128)(2,1)S(1)}, u32[]{:S(2)}, u32[]{:S(2)}) collective-permute-start(bf16[192,64]{1,0:T(8,128)(2,1)S(1)} %get-tuple-element.107), channel_id=1, source_target_pairs={{0,16},{1,17},{2,18},{3,19},{16,0},{17,1},{18,2},{19,3},{4,20},{5,... | collective-permute-start | bytes 73736 | tf_op jit(solution)/shard_map/ppermute | solution.py:246
  186.7 7.2 %collective-permute-start.10 = (bf16[192,64]{1,0:T(8,128)(2,1)S(1)}, bf16[192,64]{1,0:T(8,128)(2,1)S(1)}, u32[]{:S(2)}, u32[]{:S(2)}) collective-permute-start(bf16[192,64]{1,0:T(8,128)(2,1)S(1)} %get-tuple-element.106), channel_id=1, source_target_pairs={{0,3},{1,2},{2,1},{3,0},{16,19},{17,18},{18,17},{19,16},{4,7},{5,6... | collective-permute-start | bytes 73736 | tf_op jit(solution)/shard_map/ppermute | solution.py:246
  186.9 7.1 %collective-permute-start.9 = (bf16[192,64]{1,0:T(8,128)(2,1)S(1)}, bf16[192,64]{1,0:T(8,128)(2,1)S(1)}, u32[]{:S(2)}, u32[]{:S(2)}) collective-permute-start(bf16[192,64]{1,0:T(8,128)(2,1)S(1)} %get-tuple-element.105), channel_id=1, source_target_pairs={{0,2},{1,3},{2,0},{3,1},{16,18},{17,19},{18,16},{19,17},{4,6},{5,7... | collective-permute-start | bytes 73736 | tf_op jit(solution)/shard_map/ppermute | solution.py:246
  212.2 59.1 %all-to-all-start.3 = ((bf16[8,192,1280]{2,1,0:T(8,128)(2,1)}), bf16[8,192,1280]{2,1,0:T(8,128)(2,1)}, u32[]{:S(2)}, u32[]{:S(2)}) async-start(bf16[8,192,1280]{2,1,0:T(8,128)(2,1)} %bitcast.14), calls=%async_computation.3 | async-start | bytes 7864320 | tf_op jit(solution)/shard_map/all_to_all | solution.py:240
  244.0 26.8 %collective-permute-start.16 = (bf16[192,1024]{1,0:T(8,128)(2,1)S(1)}, bf16[192,1024]{1,0:T(8,128)(2,1)S(1)}, u32[]{:S(2)}, u32[]{:S(2)}) collective-permute-start(bf16[192,1024]{1,0:T(8,128)(2,1)S(1)} %get-tuple-element.120), channel_id=1, source_target_pairs={{0,2},{1,3},{2,0},{3,1},{16,18},{17,19},{18,16},{19,17},{4,6},{5,7... | collective-permute-start | bytes 1179656 | tf_op jit(solution)/shard_map/ppermute | solution.py:246
  245.5 32.9 %collective-permute-start.17 = (bf16[192,1024]{1,0:T(8,128)(2,1)}, bf16[192,1024]{1,0:T(8,128)(2,1)S(1)}, u32[]{:S(2)}, u32[]{:S(2)}) collective-permute-start(bf16[192,1024]{1,0:T(8,128)(2,1)} %get-tuple-element.121), channel_id=1, source_target_pairs={{0,3},{1,2},{2,1},{3,0},{16,19},{17,18},{18,17},{19,16},{4,7},{5,6... | collective-permute-start | bytes 1179656 | tf_op jit(solution)/shard_map/ppermute | solution.py:246
  245.8 32.5 %collective-permute-start.18 = (bf16[192,1024]{1,0:T(8,128)(2,1)}, bf16[192,1024]{1,0:T(8,128)(2,1)S(1)}, u32[]{:S(2)}, u32[]{:S(2)}) collective-permute-start(bf16[192,1024]{1,0:T(8,128)(2,1)} %get-tuple-element.122), channel_id=1, source_target_pairs={{0,16},{1,17},{2,18},{3,19},{16,0},{17,1},{18,2},{19,3},{4,20},{5,... | collective-permute-start | bytes 1179656 | tf_op jit(solution)/shard_map/ppermute | solution.py:246
  247.3 31.0 %collective-permute-start.19 = (bf16[192,1024]{1,0:T(8,128)(2,1)}, bf16[192,1024]{1,0:T(8,128)(2,1)S(1)}, u32[]{:S(2)}, u32[]{:S(2)}) collective-permute-start(bf16[192,1024]{1,0:T(8,128)(2,1)} %get-tuple-element.123), channel_id=1, source_target_pairs={{0,17},{1,16},{2,19},{3,18},{16,1},{17,0},{18,3},{19,2},{4,21},{5,... | collective-permute-start | bytes 1179656 | tf_op jit(solution)/shard_map/ppermute | solution.py:246
  247.5 41.1 %collective-permute-start.20 = (bf16[192,1024]{1,0:T(8,128)(2,1)}, bf16[192,1024]{1,0:T(8,128)(2,1)S(1)}, u32[]{:S(2)}, u32[]{:S(2)}) collective-permute-start(bf16[192,1024]{1,0:T(8,128)(2,1)} %get-tuple-element.124), channel_id=1, source_target_pairs={{0,18},{1,19},{2,16},{3,17},{16,2},{17,3},{18,0},{19,1},{4,22},{5,... | collective-permute-start | bytes 1179656 | tf_op jit(solution)/shard_map/ppermute | solution.py:246
  270.8 25.3 %collective-permute-start.21 = (bf16[192,1024]{1,0:T(8,128)(2,1)S(1)}, bf16[192,1024]{1,0:T(8,128)(2,1)S(1)}, u32[]{:S(2)}, u32[]{:S(2)}) collective-permute-start(bf16[192,1024]{1,0:T(8,128)(2,1)S(1)} %get-tuple-element.125), channel_id=1, source_target_pairs={{0,19},{1,18},{2,17},{3,16},{16,3},{17,2},{18,1},{19,0},{4,23},{5,... | collective-permute-start | bytes 1179656 | tf_op jit(solution)/shard_map/ppermute | solution.py:246
  (18 other events, 150.4 us)
Sparse Core Ops, SparseCore 0:
  26.3 90.0 all-gather.6
  118.0 61.0 all-gather.8
  194.0 44.1 all-gather.10

commit v4 on v3

--- a/solution.py
+++ b/solution.py
@@ -9,7 +9,6 @@
 
 LANES = 128
 CHUNK = 48
-NOTE_ROWS = 16
 SET = 8
 RANK = 64
 SCALE = 2.0
@@ -89,6 +88,7 @@
 
 def shrink_parts_kernel(ids_ref, panel_ref, *refs):
     pieces, adapters, _, width = panel_ref.shape
+    adapters -= 1
     ranks = refs[-1].shape[1]
     members = len(refs) // 2
     rows = refs[0].shape[0]
@@ -352,37 +352,25 @@
     )(array)
 
 
-def pack_kernel(steps, notes_ref, source_ref, out_ref):
+def pack_kernel(source_ref, out_ref):
     members, _, width = out_ref.shape
-
-    @pl.when(pl.program_id(0) < steps)
-    def _():
-        for m in range(members):
-            out_ref[m] = source_ref[:, m * width : (m + 1) * width]
-
-    @pl.when(pl.program_id(0) == steps)
-    def _():
-        for m in range(members):
-            out_ref[m] = notes_ref[...]
-
-
-def pack(array, notes, members):
+    for m in range(members):
+        out_ref[m] = source_ref[:, m * width : (m + 1) * width]
+
+
+def pack(array, members):
     rows, columns = array.shape
-    chunk, width = notes.shape
-    steps = rows // chunk
-    return call(
-        functools.partial(pack_kernel, steps),
+    width = columns // members
+    return call(
+        pack_kernel,
         "pack",
-        bf16(members, rows + chunk, width),
+        bf16(members, rows, width),
         0,
         4 * array.size,
-        grid=(steps + 1,),
-        in_specs=[
-            pl.BlockSpec((chunk, width), lambda i: (0, 0)),
-            pl.BlockSpec((chunk, columns), lambda i: (jnp.minimum(i, steps - 1), 0)),
-        ],
-        out_specs=pl.BlockSpec((members, chunk, width), lambda i: (0, i, 0)),
-    )(notes, array)
+        grid=(rows // CHUNK,),
+        in_specs=[pl.BlockSpec((CHUNK, columns), lambda i: (i, 0))],
+        out_specs=pl.BlockSpec((members, CHUNK, width), lambda i: (0, i, 0)),
+    )(array)
 
 
 def unpack_joint_kernel(count, inner, groups, narrow, parts_ref, q_ref, k_ref, v_ref):
@@ -453,14 +441,26 @@
     at_owner = owner[:, None] == jnp.arange(devices)[None, :]
     listed = jnp.any(fetch_list[None] == adapter_ids[:, None, None], axis=2)
     own_ids = jnp.where(jnp.any(at_owner & listed, axis=1), adapter_ids, -1)
-    notes = jnp.broadcast_to(own_ids.astype(jnp.bfloat16), (NOTE_ROWS, tok_rows))
-    notes = jnp.pad(notes, ((0, 0), (0, normed_hidden.shape[1] // devices - tok_rows)))
-    packed_x = pack(normed_hidden, notes, devices)
+    packed_x = pack(normed_hidden, devices)
     sent_x = exchange(packed_x, REQ)
 
     attn_mixed, packed_x = lax.optimization_barrier((attn_mixed, packed_x))
     sent_y = swap_parts(pack_parts(attn_mixed, p, count, inner, groups))
-    a_o = along_h(own_columns(shrink_panels[:, 3 * RANK :]))
+    own_ids, packed_x = lax.optimization_barrier((own_ids, packed_x))
+    plane_ids = lax.all_gather(own_ids[None], PLANE, axis=0, tiled=True)
+    near_ids = lax.dynamic_slice_in_dim(plane_ids, g * inner, inner, 0)
+    own_a = own_columns(shrink_panels[:, 3 * RANK :])
+    note = near_ids.astype(jnp.bfloat16)
+    note = jnp.pad(note, ((0, 0), (0, -tok_rows % own_a.shape[2])))
+    note = note.reshape(1, -1, own_a.shape[2])
+    note_rows = note.shape[1]
+    note = jnp.pad(note, ((0, 0), (0, RANK - note_rows), (0, 0)))
+    gathered = lax.all_gather(jnp.concatenate([own_a, note], axis=0), "h", axis=0)
+    group_ids = gathered[:, -1, :note_rows].reshape(count, inner, -1)[:, :, :tok_rows]
+    group_ids = group_ids.astype(jnp.int32).reshape(devices * tok_rows, 1)
+    a_o = gathered
+    if own_a.shape[2] % LANES:
+        a_o = gathered.transpose(1, 2, 0, 3).reshape((1,) + gathered.shape[1:3] + (-1,))
     own_q = own_columns(expand_qo[:, :RANK])
     fold = groups == 2 and own_q.shape[2] % LANES == 0
     if fold:
@@ -475,19 +475,9 @@
 
     sent_x, sent_y = lax.optimization_barrier((sent_x, sent_y))
 
-    group_ids = sent_x[:, tok_rows, :tok_rows].astype(jnp.int32)
-    near_ids = lax.dynamic_slice_in_dim(group_ids, h * inner, inner, 0)
-    group_ids = group_ids.reshape(devices * tok_rows, 1)
     part = shrink(group_ids, sent_x, shrink_panels, 3 * RANK, inner, tok_rows)
-    part, near_ids = lax.optimization_barrier((part, near_ids))
     near = jnp.sum(exchange(part, "r").astype(jnp.float32), axis=0).astype(jnp.bfloat16)
 
-    if groups == 2:
-        far_ids = lax.ppermute(near_ids, "groups", [(0, 1), (1, 0)])
-        first, second = jnp.where(g == 0, near_ids, far_ids), jnp.where(g == 0, far_ids, near_ids)
-        plane_ids = jnp.concatenate([first, second], axis=0)
-    else:
-        plane_ids = lax.all_gather(near_ids, "groups", axis=0, tiled=True)
     swap_ids = plane_ids[p ^ jnp.arange(members)].reshape(rows, 1)
     plane_ids = plane_ids.reshape(rows, 1)
     parts_o = shrink_parts(swap_ids, sent_y, a_o, RANK)

time: 306 us -> 301 us (0.984)
  blocking collectives: 10.4 us -> 28.7 us
  starting transfers between devices: 51.6 us -> 42.4 us
  waiting for transfers between devices: 149 us -> 140 us
    all_gather x0 -> x1, waiting for transfers between devices: none -> 28.6 us  [shards(): lax.all_gather(jnp.concatenate([own_a, note], axis=0), 'h', axis=0)]
    all_to_all x4, waiting for transfers between devices: 44.4 us -> 20.6 us  [exchange(): return lax.all_to_all(array, axes, split_axis=0, concat_axis=0, tiled=True)]
    unnamed x0 -> x1, blocking collectives: none -> 18.3 us
    ppermute x21, waiting for transfers between devices: 80.5 us -> 67.7 us  [swap_parts(): lax.ppermute(parts[s], PLANE, [(d, d ^ s) for d in range(members)])]
    all_to_all x4, starting transfers between devices: 31.4 us -> 24.3 us  [exchange(): return lax.all_to_all(array, axes, split_axis=0, concat_axis=0, tiled=True)]
    all_gather x3 -> x2, waiting for transfers between devices: 21.5 us -> 22.9 us  [along_h(): pieces = lax.all_gather(array, 'h', axis=0)]
    unnamed x29 -> x37, local copies, waits for them, and re-layouts: 12.5 us -> 11.5 us
  transfers between devices with their start and end apart: 29 -> 28, of which waited for: 12 -> 11; matrix products, arithmetic and copies ran while one was open for 7% -> 7% of each run, Pallas kernels for 13% -> 13%
where the time goes in v4:
time: 301 us; the launch traced here: 299 us
  waiting for transfers between devices  140 us (47%)
  Pallas kernels  46.5 us (15%)
  starting transfers between devices  42.4 us (14%)
  blocking collectives  28.7 us (10%)
  local copies, waits for them, and re-layouts  21.6 us (7%)
  between operations  14.7 us (5%)
  other arithmetic  5.69 us (2%)
    ppermute x21, waiting for transfers between devices, swap_parts(): lax.ppermute(parts[s], PLANE, [(d, d ^ s) for d in range(members)])  67.7 us
    all_gather x1, waiting for transfers between devices, shards(): lax.all_gather(jnp.concatenate([own_a, note], axis=0), 'h', axis=0)  28.6 us
    all_to_all x4, starting transfers between devices, exchange(): return lax.all_to_all(array, axes, split_axis=0, concat_axis=0, tiled=True)  24.3 us
    all_gather x2, waiting for transfers between devices, along_h(): pieces = lax.all_gather(array, 'h', axis=0)  22.9 us
    all_to_all x4, waiting for transfers between devices, exchange(): return lax.all_to_all(array, axes, split_axis=0, concat_axis=0, tiled=True)  20.6 us
    unnamed x1, blocking collectives  18.3 us
    ppermute x21, starting transfers between devices, swap_parts(): lax.ppermute(parts[s], PLANE, [(d, d ^ s) for d in range(members)])  18 us
    pallas_call x1, Pallas kernels, shrink(): call(functools.partial(shrink_kernel, ranks), 'shrink', bf16(inner, steps...  14.5 us
  transfers between devices with their start and end apart: 28, of which 11 were waited for; matrix products, arithmetic and copies ran while one was open for 7% of the time, Pallas kernels for 13%

profile of v4, /device:TPU:0, one launch (start us, length us, event | category | flops | bytes accessed | tf_op | source)
XLA Modules:
  0.0 299.3 jit_solution(13951198125927578416)
XLA Ops:
  7.2 4.2 %pack.1 = bf16[16,192,512]{2,1,0:T(8,128)(2,1)} custom-call(bf16[192,8192]{1,0:T(8,128)(2,1)} %source_ref.1), custom_call_target="tpu_custom_call" | custom-call | bytes 6291456 | tf_op jit(solution)/shard_map/pack/pallas_call | solution.py:364
  11.4 7.6 %all-to-all-start = ((bf16[16,192,512]{2,1,0:T(8,128)(2,1)}), bf16[16,192,512]{2,1,0:T(8,128)(2,1)}, u32[]{:S(2)}, u32[]{:S(2)}) async-start(bf16[16,192,512]{2,1,0:T(8,128)(2,1)} %pack.1), calls=%async_computation | async-start | bytes 6291456 | tf_op jit(solution)/shard_map/all_to_all | solution.py:240
  20.7 18.3 %all-reduce.2 = s32[1536]{0:T(1024)S(1)} all-reduce(s32[1536]{0:T(1024)S(1)} %dynamic-update-slice), channel_id=2, replica_groups=mesh['groups'=2,'h'=4,'r'=4] {'groups','r'}, use_global_device_ids=true, to_apply=%add.2 | all-reduce | flops 1536 | bytes 12288
  40.2 4.0 %pack_parts.1 = (bf16[192,1024]{1,0:T(8,128)(2,1)S(1)}, bf16[192,1024]{1,0:T(8,128)(2,1)S(1)}, bf16[192,1024]{1,0:T(8,128)(2,1)S(1)}, bf16[192,1024]{1,0:T(8,128...) custom-call(s32[1]{0:T(128)} %bitcast.5.p_ref, ...), custom_call_target="tpu_custom_call" | custom-call | bytes 6291456 | tf_op jit(solution)/shard_map/pack_parts/pallas_call | solution.py:284
  47.8 3.2 %fusion.5 = (bf16[16,64,512]{2,1,0:T(8,128)(2,1)}, bf16[16,64,512]{2,1,0:T(8,128)(2,1)}) fusion(bf16[16,128,512]{2,1,0:T(8,128)(2,1)} %param.15), kind=kLoop, calls=%fused_computation.27 | loop fusion | bytes 4194304 | tf_op jit(solution)/shard_map/slice | solution.py:489
  51.0 9.9 %collective-permute-done.1.refs_2_ = bf16[192,1024]{1,0:T(8,128)(2,1)S(1)} collective-permute-done((bf16[192,1024]{1,0:T(8,128)(2,1)S(1)}, bf16[192,1024]{1,0:T(8,128)(2,1)S(1)}, u32[]{:S(2)}, u32[]{:S(2)}) %collective-permute-start.1) | collective-permute-done | bytes 393248 | tf_op jit(solution)/shard_map/ppermute | solution.py:246
  72.0 17.6 %collective-permute-done.2.refs_3_ = bf16[192,1024]{1,0:T(8,128)(2,1)S(1)} collective-permute-done((bf16[192,1024]{1,0:T(8,128)(2,1)}, bf16[192,1024]{1,0:T(8,128)(2,1)S(1)}, u32[]{:S(2)}, u32[]{:S(2)}) %collective-permute-start.2) | collective-permute-done | bytes 393248 | tf_op jit(solution)/shard_map/ppermute | solution.py:246
  92.0 28.6 %all-gather.8.cloned.1.call-done = bf16[68,64,256]{2,1,0:T(8,128)(2,1)} async-done(((bf16[17,64,256]{2,1,0:T(8,128)(2,1)}), bf16[68,64,256]{2,1,0:T(8,128)(2,1)}) %all-gather.8.cloned.1.call-update) | async-done | bytes 2228240 | tf_op jit(solution)/shard_map/all_gather | solution.py:458
  122.7 14.5 %shrink.1 = bf16[4,4,192,192]{3,2,1,0:T(8,128)(2,1)} custom-call(s32[3072,1]{1,0:T(8,128)S(1)} %reshape.84.ids_ref, bf16[16,192,512]{2,1,0:T(8,128)(2,1)} %all-to-all-done.tokens_ref, bf16[16,256,512]{2,1,0:T(8,128)(2,1)} %panel_ref.1), custom_call_target="tpu_custom_call" | custom-call | flops 9663676416 | bytes 7340032 | tf_op jit(solution)/shard_map/shrink/pallas_call | solution.py:73
  137.2 4.5 %all-to-all-start.1 = ((bf16[4,4,192,192]{3,2,1,0:T(8,128)(2,1)}), bf16[4,4,192,192]{3,2,1,0:T(8,128)(2,1)}, u32[]{:S(2)}, u32[]{:S(2)}) async-start(bf16[4,4,192,192]{3,2,1,0:T(8,128)(2,1)} %shrink.1), calls=%async_computation.1 | async-start | bytes 3145728 | tf_op jit(solution)/shard_map/all_to_all | solution.py:240
  144.9 5.2 %shrink_parts.1 = (bf16[192,64]{1,0:T(8,128)(2,1)S(1)}, bf16[192,64]{1,0:T(8,128)(2,1)S(1)}, bf16[192,64]{1,0:T(8,128)(2,1)S(1)}, bf16[192,64]{1,0:T(8,128)(2,1)...) custom-call(s32[1536,1]{1,0:T(8,128)S(1)} %reshape.85.ids_ref, ...), custom_call_target="tpu_custom_call" | custom-call | flops 3422552064 | bytes 5373952 | tf_op jit(solution)/shard_map/shrink_parts/pallas_call | solution.py:112
  150.1 11.7 %all-to-all-done.1 = bf16[4,4,192,192]{3,2,1,0:T(8,128)(2,1)} async-done(((bf16[4,4,192,192]{3,2,1,0:T(8,128)(2,1)}), bf16[4,4,192,192]{3,2,1,0:T(8,128)(2,1)}, u32[]{:S(2)}, u32[]{:S(2)}) %all-to-all-start.1) | async-done | bytes 1179680 | tf_op jit(solution)/shard_map/all_to_all | solution.py:240
  161.8 2.5 reduce_sum.24
  164.4 7.7 %all-to-all-start.2 = ((bf16[4,192,192]{2,1,0:T(8,128)(2,1)}), bf16[4,192,192]{2,1,0:T(8,128)(2,1)S(1)}, u32[]{:S(2)}, u32[]{:S(2)}) async-start(bf16[4,192,192]{2,1,0:T(8,128)(2,1)} %reduce_sum.24), calls=%async_computation.2 | async-start | bytes 786432 | tf_op jit(solution)/shard_map/all_to_all | solution.py:240
  179.4 8.9 %all-to-all-done.2 = bf16[4,192,192]{2,1,0:T(8,128)(2,1)S(1)} async-done(((bf16[4,192,192]{2,1,0:T(8,128)(2,1)}), bf16[4,192,192]{2,1,0:T(8,128)(2,1)S(1)}, u32[]{:S(2)}, u32[]{:S(2)}) %all-to-all-start.2) | async-done | bytes 294944 | tf_op jit(solution)/shard_map/all_to_all | solution.py:240
  188.6 10.4 %all_gather.27.low_ref = bf16[1536,256]{1,0:T(8,128)(2,1)S(1)} all-gather(bf16[192,256]{1,0:T(8,128)(2,1)S(1)} %pad_maximum_fusion), channel_id=1, replica_groups=mesh['groups'=2,'h'=4,'r'=4] {'groups','r'}, dimensions={0}, use_global_device_ids=true | all-gather | bytes 884736 | tf_op jit(solution)/shard_map/all_gather | solution.py:492
  200.7 5.9 %expand_joint.1 = bf16[1536,1280]{1,0:T(8,128)(2,1)} custom-call(s32[1]{0:T(128)} %bitcast.g_ref, s32[1536,1]{1,0:T(8,128)S(1)} %reshape.83.ids_ref, bf16[1536,256]{1,0:T(8,128)(2,1)S(1)} %all_gather.27.low_ref, bf16[4,16,80,256]{3,2,1,0:T(8,128)(2,1)S(1)} %bitcast.15), custom_call_target="tpu_custom_call" | custom-call | flops 4026531840 | bytes 6553600 | tf_op jit(solution)/shard_map/expand_joint/pallas_call | solution.py:190
  206.6 4.5 %all-to-all-start.3 = ((bf16[8,192,1280]{2,1,0:T(8,128)(2,1)}), bf16[8,192,1280]{2,1,0:T(8,128)(2,1)}, u32[]{:S(2)}, u32[]{:S(2)}) async-start(bf16[8,192,1280]{2,1,0:T(8,128)(2,1)} %bitcast.16), calls=%async_computation.3 | async-start | bytes 7864320 | tf_op jit(solution)/shard_map/all_to_all | solution.py:240
  211.2 22.9 %all-gather.12.cloned.1.call-done = bf16[64,64,256]{2,1,0:T(8,128)(2,1)} async-done(((bf16[16,64,256]{2,1,0:T(8,128)(2,1)}), bf16[64,64,256]{2,1,0:T(8,128)(2,1)}) %all-gather.12.cloned.1.call-update) | async-done | bytes 2097168 | tf_op jit(solution)/shard_map/all_gather | solution.py:252
  234.0 5.8 %expand_parts.1 = (bf16[192,1024]{1,0:T(8,128)(2,1)S(1)}, bf16[192,1024]{1,0:T(8,128)(2,1)S(1)}, bf16[192,1024]{1,0:T(8,128)(2,1)S(1)}, bf16[192,1024]{1,0:T(8,1...) custom-call(s32[1]{0:T(128)} %bitcast.5.p_ref, ...), custom_call_target="tpu_custom_call" | custom-call | flops 3221225472 | bytes 5242880 | tf_op jit(solution)/shard_map/expand_parts/pallas_call | solution.py:228
  245.7 19.6 %collective-permute-done.15.refs_2_ = bf16[192,1024]{1,0:T(8,128)(2,1)S(1)} collective-permute-done((bf16[192,1024]{1,0:T(8,128)(2,1)S(1)}, bf16[192,1024]{1,0:T(8,128)(2,1)S(1)}, u32[]{:S(2)}, u32[]{:S(2)}) %collective-permute-start.15) | collective-permute-done | bytes 393248 | tf_op jit(solution)/shard_map/ppermute | solution.py:246
  265.8 4.6 %unpack_joint.1 = (bf16[192,8192]{1,0:T(8,128)(2,1)}, bf16[192,1024]{1,0:T(8,128)(2,1)}, bf16[192,1024]{1,0:T(8,128)(2,1)}) custom-call(bf16[8,192,1280]{2,1,0:T(8,128)(2,1)} %all-to-all-done.3.parts_ref), custom_call_target="tpu_custom_call" | custom-call | bytes 7864320 | tf_op jit(solution)/shard_map/unpack_joint/pallas_call | solution.py:395
  272.8 10.3 %collective-permute-done.19.refs_6_ = bf16[192,1024]{1,0:T(8,128)(2,1)S(1)} collective-permute-done((bf16[192,1024]{1,0:T(8,128)(2,1)}, bf16[192,1024]{1,0:T(8,128)(2,1)S(1)}, u32[]{:S(2)}, u32[]{:S(2)}) %collective-permute-start.19) | collective-permute-done | bytes 393248 | tf_op jit(solution)/shard_map/ppermute | solution.py:246
  283.1 7.5 %collective-permute-done.20.refs_7_ = bf16[192,1024]{1,0:T(8,128)(2,1)S(1)} collective-permute-done((bf16[192,1024]{1,0:T(8,128)(2,1)S(1)}, bf16[192,1024]{1,0:T(8,128)(2,1)S(1)}, u32[]{:S(2)}, u32[]{:S(2)}) %collective-permute-start.20) | collective-permute-done | bytes 393248 | tf_op jit(solution)/shard_map/ppermute | solution.py:246
  (110 shorter events, 44.8 us)
Async XLA Ops:
  11.4 111.3 %all-to-all-start = ((bf16[16,192,512]{2,1,0:T(8,128)(2,1)}), bf16[16,192,512]{2,1,0:T(8,128)(2,1)}, u32[]{:S(2)}, u32[]{:S(2)}) async-start(bf16[16,192,512]{2,1,0:T(8,128)(2,1)} %pack.1), calls=%async_computation | async-start | bytes 6291456 | tf_op jit(solution)/shard_map/all_to_all | solution.py:240
  19.0 101.6 %all-gather.8.cloned.1.call-start = ((), (), s32[]{:S(2)}) async-start(), calls=%async_computation.4 | async-start | bytes 2785280 | tf_op jit(solution)/shard_map/all_gather | solution.py:458
  40.1 158.8 %all-gather.10.cloned.1.call-start = ((), (), s32[]{:S(2)}) async-start(), calls=%async_computation.5 | async-start | bytes 3276800 | tf_op jit(solution)/shard_map/all_gather | solution.py:252
  44.3 16.7 %collective-permute-start.1 = (bf16[192,1024]{1,0:T(8,128)(2,1)S(1)}, bf16[192,1024]{1,0:T(8,128)(2,1)S(1)}, u32[]{:S(2)}, u32[]{:S(2)}) collective-permute-start(bf16[192,1024]{1,0:T(8,128)(2,1)S(1)} %get-tuple-element.66), channel_id=1, source_target_pairs={{0,2},{1,3},{2,0},{3,1},{16,18},{17,19},{18,16},{19,17},{4,6},{5,7... | collective-permute-start | bytes 1179656 | tf_op jit(solution)/shard_map/ppermute | solution.py:246
  44.3 45.3 %collective-permute-start.2 = (bf16[192,1024]{1,0:T(8,128)(2,1)}, bf16[192,1024]{1,0:T(8,128)(2,1)S(1)}, u32[]{:S(2)}, u32[]{:S(2)}) collective-permute-start(bf16[192,1024]{1,0:T(8,128)(2,1)} %get-tuple-element.67), channel_id=1, source_target_pairs={{0,3},{1,2},{2,1},{3,0},{16,19},{17,18},{18,17},{19,16},{4,7},{5,6... | collective-permute-start | bytes 1179656 | tf_op jit(solution)/shard_map/ppermute | solution.py:246
  46.1 43.5 %collective-permute-start.3 = (bf16[192,1024]{1,0:T(8,128)(2,1)}, bf16[192,1024]{1,0:T(8,128)(2,1)S(1)}, u32[]{:S(2)}, u32[]{:S(2)}) collective-permute-start(bf16[192,1024]{1,0:T(8,128)(2,1)} %get-tuple-element.68), channel_id=1, source_target_pairs={{0,16},{1,17},{2,18},{3,19},{16,0},{17,1},{18,2},{19,3},{4,20},{5,... | collective-permute-start | bytes 1179656 | tf_op jit(solution)/shard_map/ppermute | solution.py:246
  46.7 43.0 %collective-permute-start.4 = (bf16[192,1024]{1,0:T(8,128)(2,1)}, bf16[192,1024]{1,0:T(8,128)(2,1)S(1)}, u32[]{:S(2)}, u32[]{:S(2)}) collective-permute-start(bf16[192,1024]{1,0:T(8,128)(2,1)} %get-tuple-element.69), channel_id=1, source_target_pairs={{0,17},{1,16},{2,19},{3,18},{16,1},{17,0},{18,3},{19,2},{4,21},{5,... | collective-permute-start | bytes 1179656 | tf_op jit(solution)/shard_map/ppermute | solution.py:246
  51.0 39.4 %collective-permute-start.5 = (bf16[192,1024]{1,0:T(8,128)(2,1)}, bf16[192,1024]{1,0:T(8,128)(2,1)S(1)}, u32[]{:S(2)}, u32[]{:S(2)}) collective-permute-start(bf16[192,1024]{1,0:T(8,128)(2,1)} %get-tuple-element.70), channel_id=1, source_target_pairs={{0,18},{1,19},{2,16},{3,17},{16,2},{17,3},{18,0},{19,1},{4,22},{5,... | collective-permute-start | bytes 1179656 | tf_op jit(solution)/shard_map/ppermute | solution.py:246
  61.0 30.2 %collective-permute-start.6 = (bf16[192,1024]{1,0:T(8,128)(2,1)}, bf16[192,1024]{1,0:T(8,128)(2,1)S(1)}, u32[]{:S(2)}, u32[]{:S(2)}) collective-permute-start(bf16[192,1024]{1,0:T(8,128)(2,1)} %get-tuple-element.71), channel_id=1, source_target_pairs={{0,19},{1,18},{2,17},{3,16},{16,3},{17,2},{18,1},{19,0},{4,23},{5,... | collective-permute-start | bytes 1179656 | tf_op jit(solution)/shard_map/ppermute | solution.py:246
  137.2 24.6 %all-to-all-start.1 = ((bf16[4,4,192,192]{3,2,1,0:T(8,128)(2,1)}), bf16[4,4,192,192]{3,2,1,0:T(8,128)(2,1)}, u32[]{:S(2)}, u32[]{:S(2)}) async-start(bf16[4,4,192,192]{3,2,1,0:T(8,128)(2,1)} %shrink.1), calls=%async_computation.1 | async-start | bytes 3145728 | tf_op jit(solution)/shard_map/all_to_all | solution.py:240
  164.4 23.9 %all-to-all-start.2 = ((bf16[4,192,192]{2,1,0:T(8,128)(2,1)}), bf16[4,192,192]{2,1,0:T(8,128)(2,1)S(1)}, u32[]{:S(2)}, u32[]{:S(2)}) async-start(bf16[4,192,192]{2,1,0:T(8,128)(2,1)} %reduce_sum.24), calls=%async_computation.2 | async-start | bytes 786432 | tf_op jit(solution)/shard_map/all_to_all | solution.py:240
  172.0 62.0 %all-gather.12.cloned.1.call-start = ((), (), s32[]{:S(2)}) async-start(), calls=%async_computation.6 | async-start | bytes 2621440 | tf_op jit(solution)/shard_map/all_gather | solution.py:252
  173.6 14.8 %collective-permute-start.12 = (bf16[192,64]{1,0:T(8,128)(2,1)S(1)}, bf16[192,64]{1,0:T(8,128)(2,1)S(1)}, u32[]{:S(2)}, u32[]{:S(2)}) collective-permute-start(bf16[192,64]{1,0:T(8,128)(2,1)S(1)} %get-tuple-element.105), channel_id=1, source_target_pairs={{0,18},{1,19},{2,16},{3,17},{16,2},{17,3},{18,0},{19,1},{4,22},{5,... | collective-permute-start | bytes 73736 | tf_op jit(solution)/shard_map/ppermute | solution.py:246
  174.4 14.0 %collective-permute-start.13 = (bf16[192,64]{1,0:T(8,128)(2,1)S(1)}, bf16[192,64]{1,0:T(8,128)(2,1)S(1)}, u32[]{:S(2)}, u32[]{:S(2)}) collective-permute-start(bf16[192,64]{1,0:T(8,128)(2,1)S(1)} %get-tuple-element.106), channel_id=1, source_target_pairs={{0,19},{1,18},{2,17},{3,16},{16,3},{17,2},{18,1},{19,0},{4,23},{5,... | collective-permute-start | bytes 73736 | tf_op jit(solution)/shard_map/ppermute | solution.py:246
  176.4 12.0 %collective-permute-start.7 = (bf16[192,64]{1,0:T(8,128)(2,1)S(1)}, bf16[192,64]{1,0:T(8,128)(2,1)S(1)}, u32[]{:S(2)}, u32[]{:S(2)}) collective-permute-start(bf16[192,64]{1,0:T(8,128)(2,1)S(1)} %get-tuple-element.100), channel_id=1, source_target_pairs={{0,1},{1,0},{2,3},{3,2},{16,17},{17,16},{18,19},{19,18},{4,5},{5,4... | collective-permute-start | bytes 73736 | tf_op jit(solution)/shard_map/ppermute | solution.py:246
  176.7 11.8 %collective-permute-start.8 = (bf16[192,64]{1,0:T(8,128)(2,1)S(1)}, bf16[192,64]{1,0:T(8,128)(2,1)S(1)}, u32[]{:S(2)}, u32[]{:S(2)}) collective-permute-start(bf16[192,64]{1,0:T(8,128)(2,1)S(1)} %get-tuple-element.101), channel_id=1, source_target_pairs={{0,2},{1,3},{2,0},{3,1},{16,18},{17,19},{18,16},{19,17},{4,6},{5,7... | collective-permute-start | bytes 73736 | tf_op jit(solution)/shard_map/ppermute | solution.py:246
  177.4 11.1 %collective-permute-start.9 = (bf16[192,64]{1,0:T(8,128)(2,1)S(1)}, bf16[192,64]{1,0:T(8,128)(2,1)S(1)}, u32[]{:S(2)}, u32[]{:S(2)}) collective-permute-start(bf16[192,64]{1,0:T(8,128)(2,1)S(1)} %get-tuple-element.102), channel_id=1, source_target_pairs={{0,3},{1,2},{2,1},{3,0},{16,19},{17,18},{18,17},{19,16},{4,7},{5,6... | collective-permute-start | bytes 73736 | tf_op jit(solution)/shard_map/ppermute | solution.py:246
  206.6 59.1 %all-to-all-start.3 = ((bf16[8,192,1280]{2,1,0:T(8,128)(2,1)}), bf16[8,192,1280]{2,1,0:T(8,128)(2,1)}, u32[]{:S(2)}, u32[]{:S(2)}) async-start(bf16[8,192,1280]{2,1,0:T(8,128)(2,1)} %bitcast.16), calls=%async_computation.3 | async-start | bytes 7864320 | tf_op jit(solution)/shard_map/all_to_all | solution.py:240
  239.8 25.5 %collective-permute-start.15 = (bf16[192,1024]{1,0:T(8,128)(2,1)S(1)}, bf16[192,1024]{1,0:T(8,128)(2,1)S(1)}, u32[]{:S(2)}, u32[]{:S(2)}) collective-permute-start(bf16[192,1024]{1,0:T(8,128)(2,1)S(1)} %get-tuple-element.116), channel_id=1, source_target_pairs={{0,2},{1,3},{2,0},{3,1},{16,18},{17,19},{18,16},{19,17},{4,6},{5,7... | collective-permute-start | bytes 1179656 | tf_op jit(solution)/shard_map/ppermute | solution.py:246
  241.3 31.5 %collective-permute-start.16 = (bf16[192,1024]{1,0:T(8,128)(2,1)}, bf16[192,1024]{1,0:T(8,128)(2,1)S(1)}, u32[]{:S(2)}, u32[]{:S(2)}) collective-permute-start(bf16[192,1024]{1,0:T(8,128)(2,1)} %get-tuple-element.117), channel_id=1, source_target_pairs={{0,3},{1,2},{2,1},{3,0},{16,19},{17,18},{18,17},{19,16},{4,7},{5,6... | collective-permute-start | bytes 1179656 | tf_op jit(solution)/shard_map/ppermute | solution.py:246
  241.7 31.1 %collective-permute-start.17 = (bf16[192,1024]{1,0:T(8,128)(2,1)}, bf16[192,1024]{1,0:T(8,128)(2,1)S(1)}, u32[]{:S(2)}, u32[]{:S(2)}) collective-permute-start(bf16[192,1024]{1,0:T(8,128)(2,1)} %get-tuple-element.118), channel_id=1, source_target_pairs={{0,16},{1,17},{2,18},{3,19},{16,0},{17,1},{18,2},{19,3},{4,20},{5,... | collective-permute-start | bytes 1179656 | tf_op jit(solution)/shard_map/ppermute | solution.py:246
  243.1 29.7 %collective-permute-start.18 = (bf16[192,1024]{1,0:T(8,128)(2,1)}, bf16[192,1024]{1,0:T(8,128)(2,1)S(1)}, u32[]{:S(2)}, u32[]{:S(2)}) collective-permute-start(bf16[192,1024]{1,0:T(8,128)(2,1)} %get-tuple-element.119), channel_id=1, source_target_pairs={{0,17},{1,16},{2,19},{3,18},{16,1},{17,0},{18,3},{19,2},{4,21},{5,... | collective-permute-start | bytes 1179656 | tf_op jit(solution)/shard_map/ppermute | solution.py:246
  243.3 39.8 %collective-permute-start.19 = (bf16[192,1024]{1,0:T(8,128)(2,1)}, bf16[192,1024]{1,0:T(8,128)(2,1)S(1)}, u32[]{:S(2)}, u32[]{:S(2)}) collective-permute-start(bf16[192,1024]{1,0:T(8,128)(2,1)} %get-tuple-element.120), channel_id=1, source_target_pairs={{0,18},{1,19},{2,16},{3,17},{16,2},{17,3},{18,0},{19,1},{4,22},{5,... | collective-permute-start | bytes 1179656 | tf_op jit(solution)/shard_map/ppermute | solution.py:246
  265.3 25.3 %collective-permute-start.20 = (bf16[192,1024]{1,0:T(8,128)(2,1)S(1)}, bf16[192,1024]{1,0:T(8,128)(2,1)S(1)}, u32[]{:S(2)}, u32[]{:S(2)}) collective-permute-start(bf16[192,1024]{1,0:T(8,128)(2,1)S(1)} %get-tuple-element.121), channel_id=1, source_target_pairs={{0,19},{1,18},{2,17},{3,16},{16,3},{17,2},{18,1},{19,0},{4,23},{5,... | collective-permute-start | bytes 1179656 | tf_op jit(solution)/shard_map/ppermute | solution.py:246
  (20 other events, 162.3 us)
Sparse Core Ops, SparseCore 0:
  40.3 80.2 all-gather.7
  122.1 63.4 all-gather.9
  188.5 45.4 all-gather.11
